TPU v7x, 256 devices: a whole 4x4x8 slice. The times are simulated.
256 devices in a mesh: group: 16 (over x, y_lo, core), seq: 16 (over z, y_hi).
Axes of the slice: x: 4, y: 4 (y_hi: 2, y_lo: 2; y = y_hi * 2 + y_lo), z: 8, core: 2. Of those that a mesh axis runs over, the one named last changes fastest.
Arguments:
- residual: bfloat16 [16, 1024, 4608], P('group', 'seq'), may hold values from -6 to 6
- cand_qkv: bfloat16 [16, 1024, 16, 512], P('group', 'seq'), may hold values from -80 to 80
- prompt_kv: bfloat16 [16, 2048, 16, 256], P(None, 'group', 'seq'), may hold values from -4 to 4
- prompt_len: int32 [16], replicated, may hold values from 1 to 2048, 17408 in all
- cand_prompt: int32 [16], replicated, may hold values from 0 to 15, as said below
- out_weight: bfloat16 [4096, 4608], P('seq'), may hold values from -0.09375 to 0.09375
- post_gain: float32 [4608], replicated, may hold values from 0.5 to 1.5
Outputs:
- layer_out: bfloat16 [16, 1024, 4608], P('group', 'seq')
Inputs may be any that keep to these rules, and one draw needn't show every extreme that they name: `cand_prompt`: each of the 16 prompts is named by exactly one candidate.
All inputs are finite; a program needn't handle non-finite values.
Results may differ from a plain program's by a relative error of at most 0.017.
Values may be sent and summed in bfloat16 or wider, within the bound.
No kernel may reach another device: no remote copies, remote signals or barrier semaphores. Data moves between devices by JAX's collectives and lax.ppermute only.
A program may use at most 128 MiB of HBM per device.

v0:
```python
import jax
import jax.numpy as jnp
from jax import lax
from jax.sharding import PartitionSpec as P

QUERY_SCALE = 144.0 ** (-0.5)
NORM_EPS = 1e-06
NEG_FILL = -1e30


def fold_scores(running, scores, allowed, value_rows):
    old_max, old_total, old_numerator = running
    scores = jnp.where(allowed, scores, NEG_FILL)
    new_max = jnp.maximum(old_max, jnp.max(scores, axis=-1))
    weights = jnp.where(allowed, jnp.exp(scores - new_max[..., None]), 0.0)
    rescale = jnp.exp(old_max - new_max)
    new_total = old_total * rescale + jnp.sum(weights, axis=-1)
    added = jnp.einsum(
        "ctjir,crjh->ctjih",
        weights.astype(jnp.bfloat16),
        value_rows,
        preferred_element_type=jnp.float32,
    )
    new_numerator = old_numerator * rescale[..., None] + added
    return (new_max, new_total, new_numerator)


def attend_prompt(running, queries, kv_piece, limits):
    head_dim = kv_piece.shape[-1] // 2
    key_rows = kv_piece[..., :head_dim]
    value_rows = kv_piece[..., head_dim:]
    scores = (
        jnp.einsum("ctjih,crjh->ctjir", queries, key_rows, preferred_element_type=jnp.float32)
        * QUERY_SCALE
    )
    places = lax.iota(jnp.int32, kv_piece.shape[1])
    allowed = (places[None, :] < limits[:, None])[:, None, None, None, :]
    return fold_scores(running, scores, allowed, value_rows)


def body(residual, cand_qkv, prompt_kv, prompt_len, cand_prompt, out_weight, post_gain):
    seq_count = lax.axis_size("seq")
    head_dim = prompt_kv.shape[-1] // 2
    q_per_kv = cand_qkv.shape[-1] // head_dim - 2
    head_major = lax.all_to_all(cand_qkv, "seq", split_axis=2, concat_axis=1, tiled=True)
    cand_count, cand_len, kv_local = (head_major.shape[0], head_major.shape[1], head_major.shape[2])
    queries = head_major[..., : q_per_kv * head_dim].reshape(
        cand_count, cand_len, kv_local, q_per_kv, head_dim
    )
    key_rows = head_major[..., q_per_kv * head_dim : (q_per_kv + 1) * head_dim]
    value_rows = head_major[..., (q_per_kv + 1) * head_dim :]
    positions = lax.iota(jnp.int32, cand_len)
    causal = (positions[None, :] <= positions[:, None])[None, :, None, None, :]
    stat_shape = (cand_count, cand_len, kv_local, q_per_kv)
    running = (
        jnp.full(stat_shape, NEG_FILL, jnp.float32),
        jnp.zeros(stat_shape, jnp.float32),
        jnp.zeros(stat_shape + (head_dim,), jnp.float32),
    )
    own_scores = (
        jnp.einsum("ctjih,cujh->ctjiu", queries, key_rows, preferred_element_type=jnp.float32)
        * QUERY_SCALE
    )
    running = fold_scores(running, own_scores, causal, value_rows)
    own_prompts = lax.dynamic_slice_in_dim(
        cand_prompt, lax.axis_index("group") * cand_count, cand_count
    )
    picks = own_prompts[:, None] == lax.iota(jnp.int32, prompt_len.shape[0])[None, :]
    limits = jnp.sum(jnp.where(picks, prompt_len[None, :], 0), axis=1)
    running = attend_prompt(
        running,
        queries,
        lax.all_gather(prompt_kv, "group", axis=1, tiled=True)[own_prompts],
        limits,
    )
    row_max, totals, numerator = running
    attended = (numerator / totals[..., None]).astype(jnp.bfloat16)
    per_device = cand_len // seq_count
    local_rows = cand_count * per_device
    head_rows = attended.reshape(cand_count, seq_count, per_device, -1)
    head_rows = head_rows.transpose(1, 0, 2, 3).reshape(seq_count * local_rows, -1)
    projected = lax.psum_scatter(
        jnp.dot(head_rows, out_weight, preferred_element_type=jnp.float32).astype(jnp.bfloat16),
        "seq",
        scatter_dimension=0,
        tiled=True,
    ).astype(jnp.float32)
    projected = projected.reshape(cand_count, per_device, -1)
    spread = lax.rsqrt(jnp.mean(projected * projected, axis=-1, keepdims=True) + NORM_EPS)
    normed = projected * spread * post_gain
    return (residual.astype(jnp.float32) + normed).astype(jnp.bfloat16)


def solution(mesh):
    return jax.shard_map(
        body,
        mesh=mesh,
        in_specs=(
            P("group", "seq", None),
            P("group", "seq", None, None),
            P(None, "group", "seq", None),
            P(),
            P(),
            P("seq", None),
            P(),
        ),
        out_specs=P("group", "seq", None),
        check_vma=False,
    )
```

profile of v0, /device:TPU:1, one launch (start us, length us, event | category | flops | bytes accessed | tf_op | source)
XLA Modules:
  0.0 381.0 jit_solution(2399404451135324719)
XLA Ops:
  6.5 0.0 copy-start
  6.5 0.0 all-gather.2.cloned.1.call-start
  6.5 0.7 all-gather.2.cloned.1.call-update
  7.3 2.8 copy.21
  10.1 11.8 %all-to-all-start = ((bf16[1,64,16,512]{3,1,0,2:T(8,128)(2,1)}), bf16[1,64,16,512]{3,1,0,2:T(8,128)(2,1)}, u32[]{:S(2)}, u32[]{:S(2)}) async-start(bf16[1,64,16,512]{3,1,0,2:T(8,128)(2,1)} %copy.21), calls=%async_computation | async-start | bytes 2097152 | tf_op jit(solution)/shard_map/all_to_all | solution.py:45
  21.9 0.0 reduce-scatter.2.cloned.1.call-start
  21.9 1.2 dynamic_slice.3
  25.1 2.0 fusion.40
  27.1 0.7 iota_compare_fusion.1
  27.8 0.3 iota_compare_fusion
  28.2 20.6 %all-to-all-done = bf16[1,64,16,512]{3,1,0,2:T(8,128)(2,1)} async-done(((bf16[1,64,16,512]{3,1,0,2:T(8,128)(2,1)}), bf16[1,64,16,512]{3,1,0,2:T(8,128)(2,1)}, u32[]{:S(2)}, u32[]{:S(2)}) %all-to-all-start) | async-done | bytes 1048608 | tf_op jit(solution)/shard_map/all_to_all | solution.py:45
  48.7 1.9 slice.32
  50.6 2.0 copy.22
  52.6 6.2 %fusion.9 = (f32[1024,2]{0,1:T(2,128)S(1)}, f32[1024,1024,2]{1,0,2:T(8,128)}) fusion(pred[1024,1024]{0,1:T(8,128)(4,1)S(1)} %iota_compare_fusion, bf16[1024,2,128]{0,2,1:T(8,128)(2,1)} %bitcast.137, bf16[1,1024,1,512]{3,1,2,0:T(8,128)(2,1)} %bitcast.2), kind=kOutput, calls=%fused_computation.14 | convolution fusion | flops 543160320 | bytes 10231808 | tf_op jit(solution)/shard_map/ctjih,cujh->ctjiu/dot_general | solution.py:61
  58.8 58.6 %all-gather.2.cloned.1.call-done = bf16[16,2048,1,256]{3,1,2,0:T(8,128)(2,1)} async-done(((bf16[16,128,1,256]{3,1,2,0:T(8,128)(2,1)}), bf16[16,2048,1,256]{3,1,2,0:T(8,128)(2,1)}) %all-gather.2.cloned.1.call-update) | async-done | bytes 16777232 | tf_op jit(solution)/shard_map/all_gather | solution.py:73
  117.4 0.0 copy-start.1
  117.4 4.0 %bitcast_reduce_fusion = (f32[1024,2]{0,1:T(2,128)S(1)}, f32[2048,1024,2]{1,0,2:T(8,128)S(1)}) fusion(pred[2048]{0:T(1024)(128)(4,1)S(1)} %iota_compare_fusion.1, bf16[1024,2,128]{0,2,1:T(8,128)(2,1)} %bitcast.138, bf16[16,2048,1,256]{3,1,2,0:T(8,128)(2,1)} %all-gather.2.cloned.1.call-done, s32[]{:T(128)} %bitcast.16), kind=kOutput, calls=%fused_computation.1 | convolution fusion | flops 1086322688 | bytes 17836544 | tf_op jit(solution)/shard_map/ctjih,crjh->ctjir/dot_general | solution.py:33
  121.4 0.0 copy-done.1
  121.4 2.3 fusion.10
  123.7 5.1 %fusion.2 = f32[1024,2]{0,1:T(2,128)S(1)} fusion(f32[2048,1024,2]{1,0,2:T(8,128)S(1)} %get-tuple-element.24, f32[1024,2]{0,1:T(2,128)S(1)} %get-tuple-element.19, pred[2048]{0:T(1024)(128)(4,1)S(1)} %iota_compare_fusion.1), kind=kLoop, calls=%fused_computation.5 | loop fusion | flops 20969472 | bytes 16795648 | tf_op jit(solution)/shard_map/reduce_sum | solution.py:17
  128.8 3.1 fusion.28
  131.9 5.2 %divide_convert_fusion = bf16[1,1,128,1024,2]{3,2,4,1,0:T(8,128)(2,1)S(1)} fusion(f32[1,1,128,1024,2]{3,2,4,1,0:T(8,128)S(1)} %fusion.28, f32[2048,1024,2]{1,0,2:T(8,128)S(1)} %get-tuple-element.24, f32[1024,2]{0,1:T(2,128)S(1)} %get-tuple-element.19, pred[2048]{0:T(1024)(128)(4,1)S(1)} %iota_compare_fusion.1, ...), kind=kOutput, calls=%fused_computation.33 | convolution fusion | flops 1095499776 | bytes 18895364 | tf_op jit(solution)/shard_map/ctjir,crjh->ctjih/dot_general | solution.py:18
  137.2 0.0 copy-done
  137.2 0.0 copy-start.2
  137.2 0.0 copy-start.3
  137.2 5.1 %convolution_convert_fusion = bf16[1024,4608]{1,0:T(8,128)(2,1)} fusion(bf16[1024,256]{0,1:T(8,128)(2,1)S(1)} %bitcast.139, bf16[256,4608]{1,0:T(8,128)(2,1)S(1)} %copy-done), kind=kOutput, calls=%fused_computation.7 | convolution fusion | flops 2420637696 | bytes 12320768 | tf_op jit(solution)/shard_map/dot_general | solution.py:83
  142.3 0.0 reduce-scatter.2.cloned.1.call-update
  142.3 228.3 %reduce-scatter.2.cloned.1.call-done = bf16[64,4608]{1,0:T(8,128)(2,1)} async-done(((bf16[1024,4608]{1,0:T(8,128)(2,1)}), bf16[64,4608]{1,0:T(8,128)(2,1)}) %reduce-scatter.2.cloned.1.call-update) | async-done | bytes 589840 | tf_op jit(solution)/shard_map/reduce_scatter | solution.py:82
  370.6 1.3 fusion.31
  371.9 0.0 copy-done.2
  371.9 0.0 copy-done.3
  372.0 2.2 fusion.35
  (3 shorter events, 0.1 us)
Async XLA Ops:
  6.5 130.6 %copy-start = (bf16[256,4608]{1,0:T(8,128)(2,1)S(1)}, bf16[256,4608]{1,0:T(8,128)(2,1)}, u32[]{:S(2)}) copy-start(bf16[256,4608]{1,0:T(8,128)(2,1)} %param.12) | copy-start | bytes 7077892
  6.5 110.9 %all-gather.2.cloned.1.call-start = ((), (), s32[]{:S(2)}) async-start(), calls=%async_computation.2 | async-start | bytes 17825792 | tf_op jit(solution)/shard_map/all_gather | solution.py:73
  10.1 38.7 %all-to-all-start = ((bf16[1,64,16,512]{3,1,0,2:T(8,128)(2,1)}), bf16[1,64,16,512]{3,1,0,2:T(8,128)(2,1)}, u32[]{:S(2)}, u32[]{:S(2)}) async-start(bf16[1,64,16,512]{3,1,0,2:T(8,128)(2,1)} %copy.21), calls=%async_computation | async-start | bytes 2097152 | tf_op jit(solution)/shard_map/all_to_all | solution.py:45
  21.9 348.8 %reduce-scatter.2.cloned.1.call-start = ((), (), s32[]{:S(2)}) async-start(), calls=%async_computation.3 | async-start | bytes 10027008 | tf_op jit(solution)/shard_map/reduce_scatter | solution.py:82
  117.4 4.0 %copy-start.1 = (f32[1024,1024,2]{1,0,2:T(8,128)S(1)}, f32[1024,1024,2]{1,0,2:T(8,128)}, u32[]{:S(2)}) copy-start(f32[1024,1024,2]{1,0,2:T(8,128)} %get-tuple-element.22) | copy-start | bytes 25165828
  137.2 234.7 %copy-start.2 = (bf16[1,64,4608]{2,1,0:T(8,128)(2,1)S(1)}, bf16[1,64,4608]{2,1,0:T(8,128)(2,1)}, u32[]{:S(2)}) copy-start(bf16[1,64,4608]{2,1,0:T(8,128)(2,1)} %param.7) | copy-start | bytes 1769476
  137.2 234.7 %copy-start.3 = (f32[4608]{0:T(1024)S(1)}, f32[4608]{0:T(1024)}, u32[]{:S(2)}) copy-start(f32[4608]{0:T(1024)} %param.13) | copy-start | bytes 55300
Sparse Core Ops, SparseCore 0:
  9.2 108.2 all-gather.1
  142.4 228.1 reduce-scatter.1
where the time goes:
time: 385 us; the launch traced here: 381 us
  waiting for transfers between devices  308 us (80%)
  matrix products  23.6 us (6%)
  between operations  15.5 us (4%)
  other arithmetic  13.8 us (4%)
  starting transfers between devices  11.8 us (3%)
  local copies, waits for them, and re-layouts  7.97 us (2%)
    reduce_scatter x1, waiting for transfers between devices, body(): lax.psum_scatter(jnp.dot(head_rows, out_weight, preferred_element_type=jn...  228 us
    all_gather x1, waiting for transfers between devices, body(): lax.all_gather(prompt_kv, 'group', axis=1, tiled=True)[own_prompts]  58.6 us
    all_to_all x1, waiting for transfers between devices, body(): lax.all_to_all(cand_qkv, 'seq', split_axis=2, concat_axis=1, tiled=True)  20.6 us
    all_to_all x1, starting transfers between devices, body(): lax.all_to_all(cand_qkv, 'seq', split_axis=2, concat_axis=1, tiled=True)  11.8 us
    dot_general x2, matrix products, fold_scores(): jnp.einsum('ctjir,crjh->ctjih', weights.astype(jnp.bfloat16), value_rows,...  8.37 us
  transfers between devices with their start and end apart: 3, of which 3 were waited for; matrix products, arithmetic and copies ran while one was open for 5% of the time, Pallas kernels for 0%

commit v1 on v0

v1 whole, which is shorter than its diff:
```python
import functools
import math

import jax
import jax.numpy as jnp
from jax import lax
from jax.experimental import pallas as pl
from jax.experimental.pallas import tpu as pltpu
from jax.sharding import Mesh, PartitionSpec as P

QUERY_SCALE = 144.0 ** (-0.5)
EXP2_SCALE = QUERY_SCALE / math.log(2.0)
NORM_EPS = 1e-06
NEG_FILL = -1e30
GROUP = ("x", "yl", "core")
SEQ = ("z", "yh")
MIB = 1 << 20


def pick_kernel(order_ref, src_ref, dst_ref, sems):
    count = dst_ref.shape[0]
    copies = [
        pltpu.make_async_copy(src_ref.at[order_ref[i]], dst_ref.at[i], sems.at[i])
        for i in range(count)
    ]
    for copy in copies:
        copy.start()
    for copy in copies:
        copy.wait()


def pick(order, rows):
    return pl.pallas_call(
        pick_kernel,
        out_shape=jax.ShapeDtypeStruct(rows.shape, rows.dtype),
        in_specs=[
            pl.BlockSpec(memory_space=pltpu.SMEM),
            pl.BlockSpec(memory_space=pl.ANY),
        ],
        out_specs=pl.BlockSpec(memory_space=pl.ANY),
        scratch_shapes=[pltpu.SemaphoreType.DMA((rows.shape[0],))],
        name="pick_prompts",
    )(order, rows)


def attend_kernel(limit_ref, qkv_ref, kv_ref, out_ref, own_v, prompt_v, *, block):
    tokens = qkv_ref.shape[0]
    places = kv_ref.shape[0]
    hd = 128
    dims = (((1,), (1,)), ((), ()))
    own_v[:, :hd] = qkv_ref[:, 3 * hd :]
    own_v[:, hd:] = jnp.ones((tokens, hd), jnp.bfloat16)
    prompt_v[:, :hd] = kv_ref[:, hd:]
    prompt_v[:, hd:] = jnp.ones((places, hd), jnp.bfloat16)
    limit = limit_ref[0]
    prompt_bias = jnp.where(
        lax.broadcasted_iota(jnp.int32, (1, places), 1) < limit, 0.0, NEG_FILL
    ).astype(jnp.float32)
    rows = lax.broadcasted_iota(jnp.int32, (block, block), 0)
    cols = lax.broadcasted_iota(jnp.int32, (block, block), 1)
    tri = jnp.where(cols <= rows, 0.0, NEG_FILL).astype(jnp.float32)
    tri = jnp.concatenate([tri, tri], axis=0)
    for b in range(tokens // block):
        at = slice(b * block, (b + 1) * block)
        q = jnp.concatenate([qkv_ref[at, :hd], qkv_ref[at, hd : 2 * hd]], axis=0)
        score = functools.partial(
            lax.dot_general, q, dimension_numbers=dims, preferred_element_type=jnp.float32
        )
        pieces = [score(kv_ref[:, :hd]) + prompt_bias]
        values = [prompt_v[...]]
        if b > 0:
            pieces.append(score(qkv_ref[: b * block, 2 * hd : 3 * hd]))
            values.append(own_v[: b * block, :])
        pieces.append(score(qkv_ref[at, 2 * hd : 3 * hd]) + tri)
        values.append(own_v[at, :])
        top = functools.reduce(
            jnp.maximum, [jnp.max(s, axis=-1, keepdims=True) for s in pieces]
        )
        total = None
        for s, v in zip(pieces, values):
            w = jnp.exp2((s - top) * EXP2_SCALE).astype(jnp.bfloat16)
            part = jnp.dot(w, v, preferred_element_type=jnp.float32)
            total = part if total is None else total + part
        done = (total[:, :hd] / total[:, hd:]).astype(jnp.bfloat16)
        out_ref[at, :hd] = done[:block]
        out_ref[at, hd:] = done[block:]


def attend(limit, qkv, kv, block=256):
    tokens, places = qkv.shape[0], kv.shape[0]
    vmem = pl.BlockSpec(memory_space=pltpu.VMEM)
    return pl.pallas_call(
        functools.partial(attend_kernel, block=block),
        out_shape=jax.ShapeDtypeStruct((tokens, 256), jnp.bfloat16),
        in_specs=[pl.BlockSpec(memory_space=pltpu.SMEM), vmem, vmem],
        out_specs=vmem,
        scratch_shapes=[
            pltpu.VMEM((tokens, 256), jnp.bfloat16),
            pltpu.VMEM((places, 256), jnp.bfloat16),
        ],
        compiler_params=pltpu.CompilerParams(vmem_limit_bytes=40 * MIB),
        cost_estimate=pl.CostEstimate(
            flops=8 * 10**9, bytes_accessed=3 * MIB, transcendentals=6 * 10**6
        ),
        name="attend",
    )(limit, qkv, kv)


def project_kernel(spot_ref, own_ref, other_ref, w0, w1, w2, w3, send_ref, keep_ref, wbuf, sems):
    quarter = w0.shape[1]
    copies = []
    for i, w in enumerate((w0, w1, w2, w3)):
        at = pl.multiple_of(spot_ref[i] * quarter, quarter)
        copies.append(pltpu.make_async_copy(w, wbuf.at[:, pl.ds(at, quarter), :], sems.at[i]))
    for copy in copies:
        copy.start()
    blocks, half = own_ref.shape[0], own_ref.shape[1] // 2
    here = pl.multiple_of(spot_ref[4] * half, half)
    there = pl.multiple_of((1 - spot_ref[4]) * half, half)

    def stack(at):
        return [
            jnp.concatenate([own_ref[n, pl.ds(at, half), :], other_ref[n, pl.ds(at, half), :]], axis=0)
            for n in range(blocks)
        ]

    rows = [jnp.concatenate([a, b], axis=0) for a, b in zip(stack(there), stack(here))]
    for copy in copies:
        copy.wait()
    width = 256
    for j in range(wbuf.shape[2] // width):
        at = slice(j * width, (j + 1) * width)
        total = None
        for n in range(blocks):
            part = jnp.dot(rows[n], wbuf[n, :, at], preferred_element_type=jnp.float32)
            total = part if total is None else total + part
        send_ref[:, at] = total[: 2 * half].astype(jnp.bfloat16)
        keep_ref[:, at] = total[2 * half :]


def project(spots, own, other, weights):
    vmem = pl.BlockSpec(memory_space=pltpu.VMEM)
    blocks, quarter, cols = weights[0].shape
    tokens = own.shape[1]
    return pl.pallas_call(
        project_kernel,
        out_shape=(
            jax.ShapeDtypeStruct((tokens, cols), jnp.bfloat16),
            jax.ShapeDtypeStruct((tokens, cols), jnp.float32),
        ),
        in_specs=[pl.BlockSpec(memory_space=pltpu.SMEM), vmem, vmem]
        + [pl.BlockSpec(memory_space=pl.ANY)] * 4,
        out_specs=(vmem, vmem),
        scratch_shapes=[
            pltpu.VMEM((blocks, 4 * quarter, cols), jnp.bfloat16),
            pltpu.SemaphoreType.DMA((4,)),
        ],
        compiler_params=pltpu.CompilerParams(vmem_limit_bytes=40 * MIB),
        cost_estimate=pl.CostEstimate(
            flops=2 * 2 * tokens * blocks * 4 * quarter * cols,
            bytes_accessed=12 * MIB,
            transcendentals=0,
        ),
        name="project",
    )(spots, own, other, *weights)


def body(residual, cand_qkv, prompt_kv, prompt_len, cand_prompt, out_weight, post_gain):
    x, yl, core = (lax.axis_index(n) for n in GROUP)
    yh = lax.axis_index("yh")
    nx, nz = lax.axis_size("x"), lax.axis_size("z")
    group = lax.axis_index(GROUP)
    per_device, heads, width = cand_qkv.shape[1:]
    features = residual.shape[-1]
    half_cols = features // 2
    rows_here = out_weight.shape[0]
    quarter = rows_here // 4

    color = (x + 2 * yl) % 4
    piece = lax.dynamic_slice(
        out_weight, (color * quarter, core * half_cols), (quarter, half_cols)
    )
    w_own = lax.all_gather(piece, "z", axis=0, tiled=False)

    prompts = lax.all_to_all(
        pick(cand_prompt, prompt_kv.reshape(prompt_kv.shape[0], prompt_kv.shape[1], -1)),
        GROUP, 0, 0, tiled=True,
    )
    prompts = prompts.reshape(-1, prompts.shape[-1])
    by_head = cand_qkv[0].transpose(1, 0, 2)
    by_head, prompts = lax.optimization_barrier((by_head, prompts))
    qkv = lax.all_to_all(by_head, SEQ, 0, 0, tiled=True).reshape(-1, width)
    qkv, w_own = lax.optimization_barrier((qkv, w_own))

    up = [(i, (i + 1) % nx) for i in range(nx)]
    down = [(i, (i - 1) % nx) for i in range(nx)]
    swap = [(0, 1), (1, 0)]
    w_left = lax.ppermute(w_own, "x", up)
    w_right = lax.ppermute(w_own, "x", down)
    w_side = lax.ppermute(w_own, "yl", swap)

    limit = prompt_len[cand_prompt[group]].reshape(1)
    attended = attend(limit, qkv, prompts)

    own = lax.all_to_all(
        attended.reshape(nz, -1, attended.shape[-1]), "z", 0, 0, tiled=True
    )
    other = lax.ppermute(own, "core", swap)
    spots = jnp.stack([color, (color + 3) % 4, (color + 1) % 4, (color + 2) % 4, yh]).astype(jnp.int32)
    send, keep = project(spots, own, other, (w_own, w_left, w_right, w_side))
    summed = lax.ppermute(send, "yh", swap).astype(jnp.float32) + keep
    mine, theirs = summed[:per_device], summed[per_device:]
    back = lax.ppermute(theirs.astype(jnp.bfloat16), "core", swap).astype(jnp.float32)
    first = core == 0
    projected = jnp.concatenate(
        [jnp.where(first, mine, back), jnp.where(first, back, mine)], axis=1
    )
    spread = lax.rsqrt(jnp.mean(projected * projected, axis=-1, keepdims=True) + NORM_EPS)
    normed = projected * spread * post_gain
    return (residual.astype(jnp.float32) + normed[None]).astype(jnp.bfloat16)


def solution(mesh):
    fine = Mesh(mesh.devices.reshape(4, 2, 2, 8, 2), GROUP + SEQ)
    return jax.shard_map(
        body,
        mesh=fine,
        in_specs=(
            P(GROUP, SEQ, None),
            P(GROUP, SEQ, None, None),
            P(None, GROUP, SEQ, None),
            P(),
            P(),
            P(SEQ, None),
            P(),
        ),
        out_specs=P(GROUP, SEQ, None),
        check_vma=False,
    )
```

time: 385 us -> 189 us (0.49); the launches traced: 381 us -> 189 us
  waiting for transfers between devices: 308 us -> 41.9 us
  blocking collectives: 0 us -> 57.6 us
  Pallas kernels: 0 us -> 49.6 us
  matrix products: 23.6 us -> 0 us
  other arithmetic: 13.8 us -> 1.44 us
  starting transfers between devices: 11.8 us -> 18.1 us
    reduce_scatter x1 -> x0, waiting for transfers between devices: 228 us -> none  [body(): lax.psum_scatter(jnp.dot(head_rows, out_weight, preferred_element_type=jn...]
    all_gather x1, waiting for transfers between devices: 58.6 us -> 0.01 us  [body(): w_own = lax.all_gather(piece, 'z', axis=0, tiled=False)]
    all_to_all x0 -> x2, blocking collectives: none -> 57.6 us  [the longest x1 38.9 us: body(): qkv = lax.all_to_all(by_head, SEQ, 0, 0, tiled=True).reshape(-1, width)]
    pallas_call x0 -> x3, Pallas kernels: none -> 49.6 us  [the longest x1 33.7 us: pick(): pl.pallas_call(pick_kernel, out_shape=jax.ShapeDtypeStruct(rows.shape, ro...]
    ppermute x0 -> x6, waiting for transfers between devices: none -> 26.8 us  [the longest x1 12.1 us: body(): summed = lax.ppermute(send, 'yh', swap).astype(jnp.float32) + keep]
    dot_general x5 -> x0, matrix products: 23.6 us -> none  [the longest x2 8.37 us: fold_scores(): jnp.einsum('ctjir,crjh->ctjih', weights.astype(jnp.bfloat16), value_rows,...]
    ppermute x0 -> x6, starting transfers between devices: none -> 11.1 us  [the longest x1 4.99 us: body(): lax.ppermute(theirs.astype(jnp.bfloat16), 'core', swap).astype(jnp.float32)]
    reduce_sum x3 -> x0, other arithmetic: 9.35 us -> none  [the longest x2 7.32 us: fold_scores(): new_total = old_total * rescale + jnp.sum(weights, axis=-1)]
  transfers between devices with their start and end apart: 3 -> 8, of which waited for: 3 -> 7; matrix products, arithmetic and copies ran while one was open for 5% -> 1% of each run, Pallas kernels for 0% -> 23%
where the time goes in v1:
time: 189 us
  blocking collectives  57.6 us (30%)
  Pallas kernels  49.6 us (26%)
  waiting for transfers between devices  41.9 us (22%)
  starting transfers between devices  18.1 us (10%)
  between operations  15.4 us (8%)
  local copies, waits for them, and re-layouts  4.81 us (3%)
    all_to_all x1, blocking collectives, body(): qkv = lax.all_to_all(by_head, SEQ, 0, 0, tiled=True).reshape(-1, width)  38.9 us
    pallas_call x1, Pallas kernels, pick(): pl.pallas_call(pick_kernel, out_shape=jax.ShapeDtypeStruct(rows.shape, ro...  33.7 us
    all_to_all x1, blocking collectives, body(): lax.all_to_all(attended.reshape(nz, -1, attended.shape[-1]), 'z', 0, 0, t...  18.7 us
    all_to_all x1, waiting for transfers between devices, body(): lax.all_to_all(pick(cand_prompt, prompt_kv.reshape(prompt_kv.shape[0], pr...  15.1 us
    ppermute x1, waiting for transfers between devices, body(): summed = lax.ppermute(send, 'yh', swap).astype(jnp.float32) + keep  12.1 us
    ppermute x1, waiting for transfers between devices, body(): w_side = lax.ppermute(w_own, 'yl', swap)  10.6 us
    pallas_call x1, Pallas kernels, attend(): pl.pallas_call(functools.partial(attend_kernel, block=block), out_shape=j...  9.51 us
    all_to_all x1, starting transfers between devices, body(): lax.all_to_all(pick(cand_prompt, prompt_kv.reshape(prompt_kv.shape[0], pr...  6.97 us
  transfers between devices with their start and end apart: 8, of which 7 were waited for; matrix products, arithmetic and copies ran while one was open for 1% of the time, Pallas kernels for 23%

profile of v1, /device:TPU:1, one launch (start us, length us, event | category | flops | bytes accessed | tf_op | source)
XLA Modules:
  0.0 188.9 jit_solution(5839175895228945059)
XLA Ops:
  6.5 0.0 all-gather.3.cloned.1.call-start
  6.5 1.7 dynamic_slice.11
  8.2 0.0 all-gather.3.cloned.1.call-update
  8.3 33.7 %pick_prompts.1 = bf16[16,128,256]{2,1,0:T(8,128)(2,1)} custom-call(s32[16]{0:T(128)} %order_ref.1, bf16[16,128,256]{2,1,0:T(8,128)(2,1)} %bitcast.28), custom_call_target="tpu_custom_call" | custom-call | tf_op jit(solution)/shard_map/pick_prompts/pallas_call | solution.py:33
  41.9 0.0 copy-start.2
  42.0 7.0 %all-to-all-start = ((bf16[16,128,256]{2,1,0:T(8,128)(2,1)}), bf16[16,128,256]{2,1,0:T(8,128)(2,1)S(1)}, u32[]{:S(2)}, u32[]{:S(2)}) async-start(bf16[16,128,256]{2,1,0:T(8,128)(2,1)} %pick_prompts.1), calls=%async_computation | async-start | bytes 2097152 | tf_op jit(solution)/shard_map/all_to_all | solution.py:185
  48.9 0.0 copy-done.2
  48.9 0.6 copy.11
  49.5 0.0 copy-start.5
  49.5 0.0 copy-start.6
  49.5 15.1 %all-to-all-done = bf16[16,128,256]{2,1,0:T(8,128)(2,1)S(1)} async-done(((bf16[16,128,256]{2,1,0:T(8,128)(2,1)}), bf16[16,128,256]{2,1,0:T(8,128)(2,1)S(1)}, u32[]{:S(2)}, u32[]{:S(2)}) %all-to-all-start) | async-done | bytes 1048608 | tf_op jit(solution)/shard_map/all_to_all | solution.py:185
  64.6 38.9 %all_to_all.15 = bf16[16,64,512]{2,1,0:T(8,128)(2,1)} all-to-all(bf16[16,64,512]{2,1,0:T(8,128)(2,1)S(1)} %bitcast.27), channel_id=1, replica_groups=mesh['x'=4,'yl'=2,'core'=2,'z'=8,'yh'=2] {'z','yh'}, dimensions={0} | all-to-all | bytes 2097152 | tf_op jit(solution)/shard_map/all_to_all | solution.py:192
  103.6 0.0 all-gather.3.cloned.1.call-done
  103.6 0.7 collective-permute-start.3
  104.3 0.0 collective-permute-start.2
  104.3 1.5 collective-permute-start.1
  105.7 0.0 copy-done.5
  105.7 0.6 dynamic_slice.9
  108.3 0.0 copy-done.6
  108.3 0.6 dynamic_slice.10.limit_ref
  108.9 0.0 copy-start.1
  108.9 1.2 copy-done.1
  110.1 0.0 copy-start
  110.1 9.5 %attend.1 = bf16[1024,256]{1,0:T(8,128)(2,1)S(1)} custom-call(s32[1]{0:T(128)} %dynamic_slice.10.limit_ref, bf16[1024,512]{1,0:T(8,128)(2,1)S(1)} %bitcast.23, bf16[2048,256]{1,0:T(8,128)(2,1)S(1)} %bitcast.22), custom_call_target="tpu_custom_call" | custom-call | flops 8000000000 | bytes 3145728 | tf_op jit(solution)/shard_map/attend/pallas_call | solution.py:92
  119.6 18.7 %all_to_all.16.own_ref = bf16[8,128,256]{2,1,0:T(8,128)(2,1)S(1)} all-to-all(bf16[8,128,256]{2,1,0:T(8,128)(2,1)S(1)} %bitcast.24), channel_id=1, replica_groups=mesh['x'=4,'yl'=2,'core'=2,'z'=8,'yh'=2] {'z'}, dimensions={0} | all-to-all | bytes 1048576 | tf_op jit(solution)/shard_map/all_to_all | solution.py:205
  138.3 3.7 %collective-permute-start = (bf16[8,128,256]{2,1,0:T(8,128)(2,1)S(1)}, bf16[8,128,256]{2,1,0:T(8,128)(2,1)S(1)}, u32[]{:S(2)}, u32[]{:S(2)}) collective-permute-start(bf16[8,128,256]{2,1,0:T(8,128)(2,1)S(1)} %all_to_all.16.own_ref), channel_id=1, source_target_pairs={{0,16},{16,0},{1,17},{17,1},{2,18},{18,2},{3,19},{19,3},{4,20},{20... | collective-permute-start | bytes 1572872 | tf_op jit(solution)/shard_map/ppermute | solution.py:208
  142.0 0.1 stack.23.spot_ref
  142.1 1.5 collective-permute-done.other_ref
  143.5 10.6 %collective-permute-done.3.w3 = bf16[8,64,2304]{2,1,0:T(8,128)(2,1)} collective-permute-done((bf16[8,64,2304]{2,1,0:T(8,128)(2,1)}, bf16[8,64,2304]{2,1,0:T(8,128)(2,1)}, u32[]{:S(2)}, u32[]{:S(2)}) %collective-permute-start.3) | collective-permute-done | bytes 2359328 | tf_op jit(solution)/shard_map/ppermute | solution.py:200
  154.2 0.4 collective-permute-done.2.w2
  154.6 0.9 collective-permute-done.1.w1
  155.5 0.0 copy-done
  155.5 6.4 %project.1 = (bf16[128,2304]{1,0:T(8,128)(2,1)S(1)}, f32[128,2304]{1,0:T(8,128)S(1)}) custom-call(s32[5]{0:T(128)S(1)} %stack.23.spot_ref, bf16[8,128,256]{2,1,0:T(8,128)(2,1)S(1)} %all_to_all.16.own_ref, bf16[8,128,256]{2,1,0:T(8,128)(2,1)S(1)} %collective-permute-done.other_ref, bf16[8,64,2304]{2,1,0:T(8,128)(2,1)S(1)} %bitcast.21, ...), custom_call_target="tpu_custom_call" | custom-call | flops 2415919104 | bytes 12582912 | tf_op jit(solution)/shard_map/project/pallas_call | solution.py:145
  161.9 0.3 collective-permute-start.4
  162.2 12.1 %collective-permute-done.4 = bf16[128,2304]{1,0:T(8,128)(2,1)S(1)} collective-permute-done((bf16[128,2304]{1,0:T(8,128)(2,1)S(1)}, bf16[128,2304]{1,0:T(8,128)(2,1)S(1)}, u32[]{:S(2)}, u32[]{:S(2)}) %collective-permute-start.4) | collective-permute-done | bytes 589856 | tf_op jit(solution)/shard_map/ppermute | solution.py:211
  174.4 0.1 convert_add_fusion
  174.5 5.0 %collective-permute-start.5 = (bf16[64,2304]{1,0:T(8,128)(2,1)S(1)}, bf16[64,2304]{1,0:T(8,128)(2,1)S(1)}, u32[]{:S(2)}, u32[]{:S(2)}) collective-permute-start(bf16[64,2304]{1,0:T(8,128)(2,1)S(1)} %slice.14), channel_id=1, source_target_pairs={{0,16},{16,0},{1,17},{17,1},{2,18},{18,2},{3,19},{19,3},{4,20},{20... | collective-permute-start | bytes 884744 | tf_op jit(solution)/shard_map/ppermute | solution.py:213
  179.5 0.0 copy-start.3
  179.5 0.0 copy-start.4
  179.5 1.2 collective-permute-done.5
  180.7 0.1 convert_select_fusion.1
  180.8 0.2 fusion.3
  181.0 0.0 copy-done.3
  181.0 0.0 copy-done.4
  181.0 1.1 fusion.2
  (2 shorter events, 0.0 us)
Async XLA Ops:
  6.5 97.0 %all-gather.3.cloned.1.call-start = ((), (), s32[]{:S(2)}) async-start(), calls=%async_computation.3 | async-start | bytes 2654208 | tf_op jit(solution)/shard_map/all_gather | solution.py:183
  41.9 7.0 %copy-start.2 = (bf16[1,64,16,512]{3,2,1,0:T(8,128)(2,1)S(1)}, bf16[1,64,16,512]{3,2,1,0:T(8,128)(2,1)}, u32[]{:S(2)}) copy-start(bf16[1,64,16,512]{3,2,1,0:T(8,128)(2,1)} %param.8) | copy-start | bytes 3145732
  42.0 22.7 %all-to-all-start = ((bf16[16,128,256]{2,1,0:T(8,128)(2,1)}), bf16[16,128,256]{2,1,0:T(8,128)(2,1)S(1)}, u32[]{:S(2)}, u32[]{:S(2)}) async-start(bf16[16,128,256]{2,1,0:T(8,128)(2,1)} %pick_prompts.1), calls=%async_computation | async-start | bytes 2097152 | tf_op jit(solution)/shard_map/all_to_all | solution.py:185
  49.5 56.2 %copy-start.5 = (s32[16]{0:T(128)S(1)}, s32[16]{0:T(128)}, u32[]{:S(2)}) copy-start(s32[16]{0:T(128)} %order_ref.1) | copy-start | bytes 196
  49.5 58.7 %copy-start.6 = (s32[16]{0:T(128)S(1)}, s32[16]{0:T(128)}, u32[]{:S(2)}) copy-start(s32[16]{0:T(128)} %param.10) | copy-start | bytes 196
  103.6 50.6 %collective-permute-start.3 = (bf16[8,64,2304]{2,1,0:T(8,128)(2,1)}, bf16[8,64,2304]{2,1,0:T(8,128)(2,1)}, u32[]{:S(2)}, u32[]{:S(2)}) collective-permute-start(bf16[8,64,2304]{2,1,0:T(8,128)(2,1)} %bitcast.18), channel_id=1, source_target_pairs={{0,32},{32,0},{1,33},{33,1},{2,34},{34,2},{3,35},{35,3},{4,36},{36... | collective-permute-start | bytes 7077896 | tf_op jit(solution)/shard_map/ppermute | solution.py:200
  104.3 50.3 %collective-permute-start.2 = (bf16[8,64,2304]{2,1,0:T(8,128)(2,1)}, bf16[8,64,2304]{2,1,0:T(8,128)(2,1)}, u32[]{:S(2)}, u32[]{:S(2)}) collective-permute-start(bf16[8,64,2304]{2,1,0:T(8,128)(2,1)} %bitcast.19), channel_id=1, source_target_pairs={{0,192},{64,0},{128,64},{192,128},{1,193},{65,1},{129,65},{193,129... | collective-permute-start | bytes 7077896 | tf_op jit(solution)/shard_map/ppermute | solution.py:199
  104.3 51.2 %collective-permute-start.1 = (bf16[8,64,2304]{2,1,0:T(8,128)(2,1)}, bf16[8,64,2304]{2,1,0:T(8,128)(2,1)}, u32[]{:S(2)}, u32[]{:S(2)}) collective-permute-start(bf16[8,64,2304]{2,1,0:T(8,128)(2,1)} %bitcast.20), channel_id=1, source_target_pairs={{0,64},{64,128},{128,192},{192,0},{1,65},{65,129},{129,193},{193,1... | collective-permute-start | bytes 7077896 | tf_op jit(solution)/shard_map/ppermute | solution.py:198
  108.9 1.2 copy-start.1
  110.1 45.4 %copy-start = (bf16[512,2304]{1,0:T(8,128)(2,1)S(1)}, bf16[512,2304]{1,0:T(8,128)(2,1)}, u32[]{:S(2)}) copy-start(bf16[512,2304]{1,0:T(8,128)(2,1)} %all-gather.3.cloned.1.call-done) | copy-start | bytes 7077892
  138.3 5.2 %collective-permute-start = (bf16[8,128,256]{2,1,0:T(8,128)(2,1)S(1)}, bf16[8,128,256]{2,1,0:T(8,128)(2,1)S(1)}, u32[]{:S(2)}, u32[]{:S(2)}) collective-permute-start(bf16[8,128,256]{2,1,0:T(8,128)(2,1)S(1)} %all_to_all.16.own_ref), channel_id=1, source_target_pairs={{0,16},{16,0},{1,17},{17,1},{2,18},{18,2},{3,19},{19,3},{4,20},{20... | collective-permute-start | bytes 1572872 | tf_op jit(solution)/shard_map/ppermute | solution.py:208
  161.9 12.4 %collective-permute-start.4 = (bf16[128,2304]{1,0:T(8,128)(2,1)S(1)}, bf16[128,2304]{1,0:T(8,128)(2,1)S(1)}, u32[]{:S(2)}, u32[]{:S(2)}) collective-permute-start(bf16[128,2304]{1,0:T(8,128)(2,1)S(1)} %get-tuple-element.15), channel_id=1, source_target_pairs={{0,1},{1,0},{2,3},{3,2},{4,5},{5,4},{6,7},{7,6},{8,9},{9,8},{10,11... | collective-permute-start | bytes 1769480 | tf_op jit(solution)/shard_map/ppermute | solution.py:211
  174.5 6.2 %collective-permute-start.5 = (bf16[64,2304]{1,0:T(8,128)(2,1)S(1)}, bf16[64,2304]{1,0:T(8,128)(2,1)S(1)}, u32[]{:S(2)}, u32[]{:S(2)}) collective-permute-start(bf16[64,2304]{1,0:T(8,128)(2,1)S(1)} %slice.14), channel_id=1, source_target_pairs={{0,16},{16,0},{1,17},{17,1},{2,18},{18,2},{3,19},{19,3},{4,20},{20... | collective-permute-start | bytes 884744 | tf_op jit(solution)/shard_map/ppermute | solution.py:213
  179.5 1.5 copy-start.3
  179.5 1.5 copy-start.4
Sparse Core Ops, SparseCore 0:
  9.1 42.4 all-gather.2

commit v2 on v1

v2 whole, which is shorter than its diff:
```python
import functools
import math

import jax
import jax.numpy as jnp
from jax import lax
from jax.experimental import pallas as pl
from jax.experimental.pallas import tpu as pltpu
from jax.sharding import Mesh, PartitionSpec as P

QUERY_SCALE = 144.0 ** (-0.5)
EXP2_SCALE = QUERY_SCALE / math.log(2.0)
NORM_EPS = 1e-06
NEG_FILL = -1e30
GROUP = ("x", "yl", "core")
SEQ = ("z", "yh")
MIB = 1 << 20
BLOCK_LOTS = ((0, 1, -1, 2, -2, 3, -3, 4),)


def pick_kernel(order_ref, src_ref, dst_ref, sems):
    count = dst_ref.shape[0]
    copies = [
        pltpu.make_async_copy(src_ref.at[order_ref[i]], dst_ref.at[i], sems.at[i])
        for i in range(count)
    ]
    for copy in copies:
        copy.start()
    for copy in copies:
        copy.wait()


def pick(order, rows):
    return pl.pallas_call(
        pick_kernel,
        out_shape=jax.ShapeDtypeStruct(rows.shape, rows.dtype),
        in_specs=[
            pl.BlockSpec(memory_space=pltpu.SMEM),
            pl.BlockSpec(memory_space=pl.ANY),
        ],
        out_specs=pl.BlockSpec(memory_space=pltpu.VMEM),
        scratch_shapes=[pltpu.SemaphoreType.DMA((rows.shape[0],))],
        name="pick_prompts",
    )(order, rows)


def attend_kernel(spot_ref, order_ref, length_ref, qkv_ref, kv_ref, out_ref, own_v, prompt_v, *, block):
    tokens = qkv_ref.shape[0]
    places = kv_ref.shape[0]
    hd = 128
    dims = (((1,), (1,)), ((), ()))
    own_v[:, :hd] = qkv_ref[:, 3 * hd :]
    own_v[:, hd:] = jnp.ones((tokens, hd), jnp.bfloat16)
    prompt_v[:, :hd] = kv_ref[:, hd:]
    prompt_v[:, hd:] = jnp.ones((places, hd), jnp.bfloat16)
    limit = length_ref[order_ref[spot_ref[0]]]
    prompt_bias = jnp.where(
        lax.broadcasted_iota(jnp.int32, (1, places), 1) < limit, 0.0, NEG_FILL
    ).astype(jnp.float32)
    rows = lax.broadcasted_iota(jnp.int32, (block, block), 0)
    cols = lax.broadcasted_iota(jnp.int32, (block, block), 1)
    tri = jnp.where(cols <= rows, 0.0, NEG_FILL).astype(jnp.float32)
    tri = jnp.concatenate([tri, tri], axis=0)
    for b in range(tokens // block):
        at = slice(b * block, (b + 1) * block)
        q = jnp.concatenate([qkv_ref[at, :hd], qkv_ref[at, hd : 2 * hd]], axis=0)
        score = functools.partial(
            lax.dot_general, q, dimension_numbers=dims, preferred_element_type=jnp.float32
        )
        pieces = [score(kv_ref[:, :hd]) + prompt_bias]
        values = [prompt_v[...]]
        if b > 0:
            pieces.append(score(qkv_ref[: b * block, 2 * hd : 3 * hd]))
            values.append(own_v[: b * block, :])
        pieces.append(score(qkv_ref[at, 2 * hd : 3 * hd]) + tri)
        values.append(own_v[at, :])
        top = functools.reduce(
            jnp.maximum, [jnp.max(s, axis=-1, keepdims=True) for s in pieces]
        )
        total = None
        for s, v in zip(pieces, values):
            w = jnp.exp2((s - top) * EXP2_SCALE).astype(jnp.bfloat16)
            part = jnp.dot(w, v, preferred_element_type=jnp.float32)
            total = part if total is None else total + part
        done = total[:, :hd] / total[:, hd:]
        done = jnp.concatenate([done[:block], done[block:]], axis=1)
        out_ref[at, :] = pltpu.roll(done, spot_ref[1], 1).astype(jnp.bfloat16)


def attend(spots, order, lengths, qkv, kv, block=256):
    tokens, places = qkv.shape[0], kv.shape[0]
    vmem = pl.BlockSpec(memory_space=pltpu.VMEM)
    return pl.pallas_call(
        functools.partial(attend_kernel, block=block),
        out_shape=jax.ShapeDtypeStruct((tokens, 256), jnp.bfloat16),
        in_specs=[pl.BlockSpec(memory_space=pltpu.SMEM)] * 3 + [vmem, vmem],
        out_specs=vmem,
        scratch_shapes=[
            pltpu.VMEM((tokens, 256), jnp.bfloat16),
            pltpu.VMEM((places, 256), jnp.bfloat16),
        ],
        compiler_params=pltpu.CompilerParams(vmem_limit_bytes=32 * MIB),
        cost_estimate=pl.CostEstimate(
            flops=10**6, bytes_accessed=MIB // 16, transcendentals=0
        ),
        name="attend",
    )(spots, order, lengths, qkv, kv)


def project_kernel(spot_ref, own_ref, other_ref, *refs):
    weights, (send_ref, keep_ref, total) = refs[:-3], refs[-3:]
    blocks = own_ref.shape[0]
    cols = keep_ref.shape[1]
    half = own_ref.shape[1] // 2
    here = pl.multiple_of(spot_ref[0] * half, half)
    there = pl.multiple_of((1 - spot_ref[0]) * half, half)
    width = 256
    places = [(lot, k) for lot in range(len(weights) // 4) for k in range(weights[4 * lot].shape[0])]
    for r, (lot, k) in enumerate(places):
        n = lax.rem(spot_ref[1] + BLOCK_LOTS[lot][k] + blocks, blocks)
        tokens = jnp.concatenate(
            [ref[n, pl.ds(at, half), :] for at in (there, here) for ref in (own_ref, other_ref)],
            axis=0,
        )
        for j in range(cols // width):
            at = slice(j * width, (j + 1) * width)
            block = jnp.concatenate([weights[4 * lot + i][k, :, at] for i in range(4)], axis=0)
            part = jnp.dot(tokens, block, preferred_element_type=jnp.float32)
            if r > 0:
                part = part + total[:, at]
            if r < blocks - 1:
                total[:, at] = part
            else:
                send_ref[:, at] = part[: 2 * half].astype(jnp.bfloat16)
                keep_ref[:, at] = part[2 * half :]


def project(spots, own, other, weights):
    vmem = pl.BlockSpec(memory_space=pltpu.VMEM)
    quarter, cols = weights[0].shape[1:]
    blocks, tokens = own.shape[:2]
    return pl.pallas_call(
        project_kernel,
        out_shape=(
            jax.ShapeDtypeStruct((tokens, cols), jnp.bfloat16),
            jax.ShapeDtypeStruct((tokens, cols), jnp.float32),
        ),
        in_specs=[pl.BlockSpec(memory_space=pltpu.SMEM)] + [vmem] * (2 + len(weights)),
        out_specs=(vmem, vmem),
        scratch_shapes=[pltpu.VMEM((2 * tokens, cols), jnp.float32)],
        compiler_params=pltpu.CompilerParams(vmem_limit_bytes=32 * MIB),
        cost_estimate=pl.CostEstimate(
            flops=2 * 2 * tokens * blocks * 4 * quarter * cols,
            bytes_accessed=12 * MIB,
            transcendentals=0,
        ),
        name="project",
    )(spots, own, other, *weights)


def body(residual, cand_qkv, prompt_kv, prompt_len, cand_prompt, out_weight, post_gain):
    x, yl, core = (lax.axis_index(n) for n in GROUP)
    yh = lax.axis_index("yh")
    nx, nz = lax.axis_size("x"), lax.axis_size("z")
    group = lax.axis_index(GROUP)
    per_device, heads, width = cand_qkv.shape[1:]
    features = residual.shape[-1]
    half_cols = features // 2
    rows_here = out_weight.shape[0]
    quarter = rows_here // 4

    color = (x + 2 * yl) % 4
    piece = lax.dynamic_slice(
        out_weight, (color * quarter, core * half_cols), (quarter, half_cols)
    )
    def from_z(block, distance):
        return lax.ppermute(block, "z", [((i + distance) % nz, i) for i in range(nz)])

    def from_sides(lot):
        return [
            lot,
            lax.ppermute(lot, "x", [(i, (i - 1) % nx) for i in range(nx)]),
            lax.ppermute(lot, "yl", swap),
            lax.ppermute(lot, "x", [(i, (i + 1) % nx) for i in range(nx)]),
        ]

    swap = [(0, 1), (1, 0)]
    blocks = {0: piece, **{d: from_z(piece, d) for d in (1, -1, 2, -2)}}
    blocks.update({3: from_z(blocks[2], 1), -3: from_z(blocks[-2], -1)})
    blocks[4] = from_z(blocks[3], 1)
    lots = [jnp.stack([blocks[d] for d in lot]) for lot in BLOCK_LOTS]
    picked = pick(cand_prompt, prompt_kv.reshape(prompt_kv.shape[0], prompt_kv.shape[1], -1))
    prompts = lax.all_to_all(picked, GROUP, 0, 0, tiled=True)
    prompts = prompts.reshape(-1, prompts.shape[-1])
    by_head = cand_qkv[0].transpose(1, 0, 2)
    by_head, prompts, lots = lax.optimization_barrier((by_head, prompts, lots))
    qkv = lax.all_to_all(by_head, SEQ, 0, 0, tiled=True).reshape(-1, width)
    weights = from_sides(lots[0])

    turn = (4 - color) % 4 * quarter
    attended = attend(
        jnp.stack([group, turn]).astype(jnp.int32), cand_prompt, prompt_len, qkv, prompts
    )
    own = lax.all_to_all(
        attended.reshape(nz, -1, attended.shape[-1]), "z", 0, 0, tiled=True
    )
    other = lax.ppermute(own, "core", swap)
    spots = jnp.stack([yh, lax.axis_index("z")]).astype(jnp.int32)
    send, keep = project(spots, own, other, weights)
    summed = lax.ppermute(send, "yh", swap).astype(jnp.float32) + keep
    mine, theirs = summed[:per_device], summed[per_device:]
    back = lax.ppermute(theirs.astype(jnp.bfloat16), "core", swap).astype(jnp.float32)
    first = core == 0
    projected = jnp.concatenate(
        [jnp.where(first, mine, back), jnp.where(first, back, mine)], axis=1
    )
    spread = lax.rsqrt(jnp.mean(projected * projected, axis=-1, keepdims=True) + NORM_EPS)
    normed = projected * spread * post_gain
    return (residual.astype(jnp.float32) + normed[None]).astype(jnp.bfloat16)


def solution(mesh):
    fine = Mesh(mesh.devices.reshape(4, 2, 2, 8, 2), GROUP + SEQ)
    return jax.shard_map(
        body,
        mesh=fine,
        in_specs=(
            P(GROUP, SEQ, None),
            P(GROUP, SEQ, None, None),
            P(None, GROUP, SEQ, None),
            P(),
            P(),
            P(SEQ, None),
            P(),
        ),
        out_specs=P(GROUP, SEQ, None),
        check_vma=False,
    )
```

time: 189 us -> 143 us (0.76)
  blocking collectives: 57.6 us -> 23.2 us
  Pallas kernels: 49.6 us -> 18.2 us
  starting transfers between devices: 18.1 us -> 41.4 us
  between operations: 15.4 us -> 0.17 us
  local copies, waits for them, and re-layouts: 4.81 us -> 11.7 us
  waiting for transfers between devices: 41.9 us -> 45.8 us
    all_to_all x1 -> x0, blocking collectives: 38.9 us -> none  [body(): qkv = lax.all_to_all(by_head, SEQ, 0, 0, tiled=True).reshape(-1, width)]
    pallas_call x1, Pallas kernels: 33.7 us -> 3.02 us  [pick(): pl.pallas_call(pick_kernel, out_shape=jax.ShapeDtypeStruct(rows.shape, ro...]
    ppermute x3 -> x10, starting transfers between devices: 2.17 us -> 18.7 us  [the longest x7 15.5 us: from_z(): lax.ppermute(block, 'z', [((i + distance) % nz, i) for i in range(nz)])]
    unnamed x15 -> x20, local copies, waits for them, and re-layouts: 1.83 us -> 11.6 us
    all_to_all x1 -> x2, waiting for transfers between devices: 15.1 us -> 22.7 us  [the longest x1 22.7 us: body(): qkv = lax.all_to_all(by_head, SEQ, 0, 0, tiled=True).reshape(-1, width)]
    all_to_all x1 -> x2, starting transfers between devices: 6.97 us -> 14.3 us  [the longest x1 7.42 us: body(): qkv = lax.all_to_all(by_head, SEQ, 0, 0, tiled=True).reshape(-1, width)]
    all_to_all x1, blocking collectives: 18.7 us -> 23.2 us  [body(): lax.all_to_all(attended.reshape(nz, -1, attended.shape[-1]), 'z', 0, 0, t...]
    dynamic_slice x3 -> x0, local copies, waits for them, and re-layouts: 2.86 us -> none  [the longest x1 1.69 us: body(): lax.dynamic_slice(out_weight, (color * quarter, core * half_cols), (quart...]
  transfers between devices with their start and end apart: 8 -> 15, of which waited for: 7 -> 8; matrix products, arithmetic and copies ran while one was open for 1% -> 5% of each run, Pallas kernels for 23% -> 9%
where the time goes in v2:
time: 143 us; the launch traced here: 142 us
  waiting for transfers between devices  45.8 us (32%)
  starting transfers between devices  41.4 us (29%)
  blocking collectives  23.2 us (16%)
  Pallas kernels  18.2 us (13%)
  local copies, waits for them, and re-layouts  11.7 us (8%)
  other arithmetic  1.6 us (1%)
    all_to_all x1, blocking collectives, body(): lax.all_to_all(attended.reshape(nz, -1, attended.shape[-1]), 'z', 0, 0, t...  23.2 us
    all_to_all x1, waiting for transfers between devices, body(): qkv = lax.all_to_all(by_head, SEQ, 0, 0, tiled=True).reshape(-1, width)  22.7 us
    ppermute x7, starting transfers between devices, from_z(): lax.ppermute(block, 'z', [((i + distance) % nz, i) for i in range(nz)])  15.5 us
    unnamed x20, local copies, waits for them, and re-layouts  11.6 us
    ppermute x1, waiting for transfers between devices, body(): summed = lax.ppermute(send, 'yh', swap).astype(jnp.float32) + keep  11.2 us
    pallas_call x1, Pallas kernels, attend(): pl.pallas_call(functools.partial(attend_kernel, block=block), out_shape=j...  9.46 us
    ppermute x7, waiting for transfers between devices, from_z(): lax.ppermute(block, 'z', [((i + distance) % nz, i) for i in range(nz)])  8.43 us
    all_to_all x1, starting transfers between devices, body(): qkv = lax.all_to_all(by_head, SEQ, 0, 0, tiled=True).reshape(-1, width)  7.42 us
  transfers between devices with their start and end apart: 15, of which 8 were waited for; matrix products, arithmetic and copies ran while one was open for 5% of the time, Pallas kernels for 9%

profile of v2, /device:TPU:1, one launch (start us, length us, event | category | flops | bytes accessed | tf_op | source)
XLA Modules:
  0.0 142.0 jit_solution(5356471118643570054)
XLA Ops:
  0.0 1.7 %bitcast_dynamic-update-slice_fusion.7 = (bf16[8,64,2304]{2,1,0:T(8,128)(2,1)S(1)}, bf16[64,2304]{1,0:T(8,128)(2,1)}) fusion(bf16[256,4608]{1,0:T(8,128)(2,1)} %param.12, s32[]{:T(128)S(6)} %select_n.32, s32[]{:T(128)S(6)} %select_n.33), kind=kLoop, calls=%fused_computation.18 | loop fusion | bytes 884744
  1.7 6.8 %collective-permute-start.2 = (bf16[64,2304]{1,0:T(8,128)(2,1)}, bf16[64,2304]{1,0:T(8,128)(2,1)}, u32[]{:S(2)}, u32[]{:S(2)}) collective-permute-start(bf16[64,2304]{1,0:T(8,128)(2,1)} %get-tuple-element.16), channel_id=1, source_target_pairs={{4,0},{6,2},{8,4},{10,6},{12,8},{14,10},{0,12},{2,14},{5,1},{7,3},... | collective-permute-start | bytes 884744 | tf_op jit(solution)/shard_map/ppermute | solution.py:177
  8.6 0.7 collective-permute-start
  9.3 0.7 collective-permute-start.1
  10.0 0.5 collective-permute-start.3
  10.5 3.0 %pick_prompts.1 = bf16[16,128,256]{2,1,0:T(8,128)(2,1)} custom-call(s32[16]{0:T(128)} %order_ref.3, bf16[16,128,256]{2,1,0:T(8,128)(2,1)} %bitcast.37), custom_call_target="tpu_custom_call" | custom-call | tf_op jit(solution)/shard_map/pick_prompts/pallas_call | solution.py:34
  13.5 6.9 %all-to-all-start = ((bf16[16,128,256]{2,1,0:T(8,128)(2,1)}), bf16[16,128,256]{2,1,0:T(8,128)(2,1)S(1)}, u32[]{:S(2)}, u32[]{:S(2)}) async-start(bf16[16,128,256]{2,1,0:T(8,128)(2,1)} %pick_prompts.1), calls=%async_computation | async-start | bytes 2097152 | tf_op jit(solution)/shard_map/all_to_all | solution.py:193
  20.4 2.8 %copy.11 = bf16[1,64,16,512]{3,1,2,0:T(8,128)(2,1)} copy(bf16[1,64,16,512]{3,2,1,0:T(8,128)(2,1)} %param.8) | data formatting | bytes 2097152 | tf_op args[1]
  23.2 0.0 collective-permute-done.2
  23.2 3.0 %collective-permute-start.4 = (bf16[64,2304]{1,0:T(8,128)(2,1)}, bf16[64,2304]{1,0:T(8,128)(2,1)S(1)}, u32[]{:S(2)}, u32[]{:S(2)}) collective-permute-start(bf16[64,2304]{1,0:T(8,128)(2,1)} %collective-permute-done.2), channel_id=1, source_target_pairs={{2,0},{4,2},{6,4},{8,6},{10,8},{12,10},{14,12},{0,14},{3,1},{5,3},... | collective-permute-start | bytes 884744 | tf_op jit(solution)/shard_map/ppermute | solution.py:177
  26.2 1.8 %collective-permute-done = bf16[64,2304]{1,0:T(8,128)(2,1)} collective-permute-done((bf16[64,2304]{1,0:T(8,128)(2,1)}, bf16[64,2304]{1,0:T(8,128)(2,1)}, u32[]{:S(2)}, u32[]{:S(2)}) %collective-permute-start) | collective-permute-done | bytes 294944 | tf_op jit(solution)/shard_map/ppermute | solution.py:177
  27.9 1.0 bitcast_dynamic-update-slice_fusion.6
  28.9 0.0 collective-permute-done.1
  28.9 1.0 bitcast_dynamic-update-slice_fusion.5
  29.9 1.0 bitcast_dynamic-update-slice_fusion.4
  30.9 0.0 copy-start.2
  30.9 0.0 copy-start.3
  30.9 0.0 collective-permute-done.3
  30.9 0.7 collective-permute-start.5
  31.6 1.0 bitcast_dynamic-update-slice_fusion.3
  32.6 1.5 %collective-permute-done.4 = bf16[64,2304]{1,0:T(8,128)(2,1)S(1)} collective-permute-done((bf16[64,2304]{1,0:T(8,128)(2,1)}, bf16[64,2304]{1,0:T(8,128)(2,1)S(1)}, u32[]{:S(2)}, u32[]{:S(2)}) %collective-permute-start.4) | collective-permute-done | bytes 294944 | tf_op jit(solution)/shard_map/ppermute | solution.py:177
  34.2 3.1 %collective-permute-start.6 = (bf16[64,2304]{1,0:T(8,128)(2,1)S(1)}, bf16[64,2304]{1,0:T(8,128)(2,1)S(1)}, u32[]{:S(2)}, u32[]{:S(2)}) collective-permute-start(bf16[64,2304]{1,0:T(8,128)(2,1)S(1)} %collective-permute-done.4), channel_id=1, source_target_pairs={{2,0},{4,2},{6,4},{8,6},{10,8},{12,10},{14,12},{0,14},{3,1},{5,3},... | collective-permute-start | bytes 884744 | tf_op jit(solution)/shard_map/ppermute | solution.py:177
  37.3 2.5 %collective-permute-done.5 = bf16[64,2304]{1,0:T(8,128)(2,1)S(1)} collective-permute-done((bf16[64,2304]{1,0:T(8,128)(2,1)}, bf16[64,2304]{1,0:T(8,128)(2,1)S(1)}, u32[]{:S(2)}, u32[]{:S(2)}) %collective-permute-start.5) | collective-permute-done | bytes 294944 | tf_op jit(solution)/shard_map/ppermute | solution.py:177
  39.8 2.6 %collective-permute-done.6 = bf16[64,2304]{1,0:T(8,128)(2,1)S(1)} collective-permute-done((bf16[64,2304]{1,0:T(8,128)(2,1)S(1)}, bf16[64,2304]{1,0:T(8,128)(2,1)S(1)}, u32[]{:S(2)}, u32[]{:S(2)}) %collective-permute-start.6) | collective-permute-done | bytes 294944 | tf_op jit(solution)/shard_map/ppermute | solution.py:177
  42.4 0.0 copy-start
  42.4 0.0 all-to-all-done
  42.4 1.4 %copy-done = bf16[8,64,2304]{2,1,0:T(8,128)(2,1)} copy-done((bf16[8,64,2304]{2,1,0:T(8,128)(2,1)}, bf16[8,64,2304]{2,1,0:T(8,128)(2,1)S(1)}, u32[]{:S(2)}) %copy-start) | copy-done | bytes 2359320
  43.9 7.4 %all-to-all-start.1 = ((bf16[16,64,512]{2,1,0:T(8,128)(2,1)}), bf16[16,64,512]{2,1,0:T(8,128)(2,1)S(1)}, u32[]{:S(2)}, u32[]{:S(2)}) async-start(bf16[16,64,512]{2,1,0:T(8,128)(2,1)} %bitcast.36), calls=%async_computation.1 | async-start | bytes 2097152 | tf_op jit(solution)/shard_map/all_to_all | solution.py:197
  51.3 1.3 collective-permute-start.10
  52.6 0.4 collective-permute-start.9
  53.0 1.5 %collective-permute-start.8 = (bf16[8,64,2304]{2,1,0:T(8,128)(2,1)}, bf16[8,64,2304]{2,1,0:T(8,128)(2,1)}, u32[]{:S(2)}, u32[]{:S(2)}) collective-permute-start(bf16[8,64,2304]{2,1,0:T(8,128)(2,1)} %copy-done), channel_id=1, source_target_pairs={{0,192},{64,0},{128,64},{192,128},{1,193},{65,1},{129,65},{193,129... | collective-permute-start | bytes 7077896 | tf_op jit(solution)/shard_map/ppermute | solution.py:182
  54.4 0.1 pad_add_fusion.1.spot_ref
  54.5 22.7 %all-to-all-done.1 = bf16[16,64,512]{2,1,0:T(8,128)(2,1)S(1)} async-done(((bf16[16,64,512]{2,1,0:T(8,128)(2,1)}), bf16[16,64,512]{2,1,0:T(8,128)(2,1)S(1)}, u32[]{:S(2)}, u32[]{:S(2)}) %all-to-all-start.1) | async-done | bytes 1048608 | tf_op jit(solution)/shard_map/all_to_all | solution.py:197
  77.2 0.0 copy-done.2
  77.2 0.0 copy-done.3
  77.2 9.5 %attend.1 = bf16[1024,256]{1,0:T(8,128)(2,1)S(1)} custom-call(s32[2]{0:T(128)S(1)} %pad_add_fusion.1.spot_ref, s32[16]{0:T(128)S(1)} %copy-done.2, s32[16]{0:T(128)S(1)} %copy-done.3, bf16[1024,512]{1,0:T(8,128)(2,1)S(1)} %bitcast.32, bf16[2048,256]{1,0:T(8,128)(2,1)S(1)} %bitcast.31), custom_call_target="tpu_custom_call" | custom-call | flops 1000000 | bytes 65536 | tf_op jit(solution)/shard_map/attend/pallas_call | solution.py:93
  86.7 23.2 %all_to_all.15.own_ref = bf16[8,128,256]{2,1,0:T(8,128)(2,1)S(1)} all-to-all(bf16[8,128,256]{2,1,0:T(8,128)(2,1)S(1)} %bitcast.33), channel_id=1, replica_groups=mesh['x'=4,'yl'=2,'core'=2,'z'=8,'yh'=2] {'z'}, dimensions={0} | all-to-all | bytes 1048576 | tf_op jit(solution)/shard_map/all_to_all | solution.py:204
  109.8 2.2 %collective-permute-start.7 = (bf16[8,128,256]{2,1,0:T(8,128)(2,1)S(1)}, bf16[8,128,256]{2,1,0:T(8,128)(2,1)S(1)}, u32[]{:S(2)}, u32[]{:S(2)}) collective-permute-start(bf16[8,128,256]{2,1,0:T(8,128)(2,1)S(1)} %all_to_all.15.own_ref), channel_id=1, source_target_pairs={{0,16},{16,0},{1,17},{17,1},{2,18},{18,2},{3,19},{19,3},{4,20},{20... | collective-permute-start | bytes 1572872 | tf_op jit(solution)/shard_map/ppermute | solution.py:207
  112.1 0.1 pad_add_fusion.spot_ref
  112.1 0.0 collective-permute-done.10.refs_3_
  112.1 2.3 %collective-permute-done.9.refs_2_ = bf16[8,64,2304]{2,1,0:T(8,128)(2,1)} collective-permute-done((bf16[8,64,2304]{2,1,0:T(8,128)(2,1)}, bf16[8,64,2304]{2,1,0:T(8,128)(2,1)}, u32[]{:S(2)}, u32[]{:S(2)}) %collective-permute-start.9) | collective-permute-done | bytes 2359328 | tf_op jit(solution)/shard_map/ppermute | solution.py:183
  114.5 0.0 collective-permute-done.8.refs_1_
  114.5 0.0 collective-permute-done.7.other_ref
  114.5 0.0 copy-start.1
  114.5 1.7 %copy-done.1 = bf16[8,64,2304]{2,1,0:T(8,128)(2,1)S(1)} copy-done((bf16[8,64,2304]{2,1,0:T(8,128)(2,1)S(1)}, bf16[8,64,2304]{2,1,0:T(8,128)(2,1)}, u32[]{:S(2)}) %copy-start.1) | copy-done | bytes 2359320
  116.1 5.7 %project.1 = (bf16[128,2304]{1,0:T(8,128)(2,1)S(1)}, f32[128,2304]{1,0:T(8,128)S(1)}) custom-call(s32[2]{0:T(128)S(1)} %pad_add_fusion.spot_ref, bf16[8,128,256]{2,1,0:T(8,128)(2,1)S(1)} %all_to_all.15.own_ref, bf16[8,128,256]{2,1,0:T(8,128)(2,1)S(1)} %collective-permute-done.7.other_ref, bf16[8,64,2304]{2,1,0:T(8,128)(2,1)S(1)} %copy-done.1, ...), custom_call_target="tpu_custom_call" | custom-call | flops 2415919104 | bytes 12582912 | tf_op jit(solution)/shard_map/project/pallas_call | solution.py:142
  121.9 2.6 %collective-permute-start.11 = (bf16[128,2304]{1,0:T(8,128)(2,1)S(1)}, bf16[128,2304]{1,0:T(8,128)(2,1)S(1)}, u32[]{:S(2)}, u32[]{:S(2)}) collective-permute-start(bf16[128,2304]{1,0:T(8,128)(2,1)S(1)} %get-tuple-element.13), channel_id=1, source_target_pairs={{0,1},{1,0},{2,3},{3,2},{4,5},{5,4},{6,7},{7,6},{8,9},{9,8},{10,11... | collective-permute-start | bytes 1769480 | tf_op jit(solution)/shard_map/ppermute | solution.py:210
  124.5 11.2 %collective-permute-done.11 = bf16[128,2304]{1,0:T(8,128)(2,1)S(1)} collective-permute-done((bf16[128,2304]{1,0:T(8,128)(2,1)S(1)}, bf16[128,2304]{1,0:T(8,128)(2,1)S(1)}, u32[]{:S(2)}, u32[]{:S(2)}) %collective-permute-start.11) | collective-permute-done | bytes 589856 | tf_op jit(solution)/shard_map/ppermute | solution.py:210
  135.6 0.1 convert_add_fusion
  135.7 0.0 copy-start.4
  135.8 0.0 copy-start.5
  135.8 3.6 %collective-permute-start.12 = (bf16[64,2304]{1,0:T(8,128)(2,1)S(1)}, bf16[64,2304]{1,0:T(8,128)(2,1)S(1)}, u32[]{:S(2)}, u32[]{:S(2)}) collective-permute-start(bf16[64,2304]{1,0:T(8,128)(2,1)S(1)} %slice.14), channel_id=1, source_target_pairs={{0,16},{16,0},{1,17},{17,1},{2,18},{18,2},{3,19},{19,3},{4,20},{20... | collective-permute-start | bytes 884744 | tf_op jit(solution)/shard_map/ppermute | solution.py:212
  139.5 1.2 collective-permute-done.12
  140.7 0.1 convert_select_fusion.1
  140.7 0.2 fusion.3
  140.9 0.0 copy-done.4
  141.0 0.0 copy-done.5
  141.0 1.1 fusion.2
  (5 shorter events, 0.1 us)
Async XLA Ops:
  1.7 21.5 %collective-permute-start.2 = (bf16[64,2304]{1,0:T(8,128)(2,1)}, bf16[64,2304]{1,0:T(8,128)(2,1)}, u32[]{:S(2)}, u32[]{:S(2)}) collective-permute-start(bf16[64,2304]{1,0:T(8,128)(2,1)} %get-tuple-element.16), channel_id=1, source_target_pairs={{4,0},{6,2},{8,4},{10,6},{12,8},{14,10},{0,12},{2,14},{5,1},{7,3},... | collective-permute-start | bytes 884744 | tf_op jit(solution)/shard_map/ppermute | solution.py:177
  8.6 19.4 %collective-permute-start = (bf16[64,2304]{1,0:T(8,128)(2,1)}, bf16[64,2304]{1,0:T(8,128)(2,1)}, u32[]{:S(2)}, u32[]{:S(2)}) collective-permute-start(bf16[64,2304]{1,0:T(8,128)(2,1)} %get-tuple-element.16), channel_id=1, source_target_pairs={{2,0},{4,2},{6,4},{8,6},{10,8},{12,10},{14,12},{0,14},{3,1},{5,3},... | collective-permute-start | bytes 884744 | tf_op jit(solution)/shard_map/ppermute | solution.py:177
  9.3 19.6 %collective-permute-start.1 = (bf16[64,2304]{1,0:T(8,128)(2,1)}, bf16[64,2304]{1,0:T(8,128)(2,1)}, u32[]{:S(2)}, u32[]{:S(2)}) collective-permute-start(bf16[64,2304]{1,0:T(8,128)(2,1)} %get-tuple-element.16), channel_id=1, source_target_pairs={{14,0},{0,2},{2,4},{4,6},{6,8},{8,10},{10,12},{12,14},{15,1},{1,3}... | collective-permute-start | bytes 884744 | tf_op jit(solution)/shard_map/ppermute | solution.py:177
  10.0 20.9 %collective-permute-start.3 = (bf16[64,2304]{1,0:T(8,128)(2,1)}, bf16[64,2304]{1,0:T(8,128)(2,1)}, u32[]{:S(2)}, u32[]{:S(2)}) collective-permute-start(bf16[64,2304]{1,0:T(8,128)(2,1)} %get-tuple-element.16), channel_id=1, source_target_pairs={{12,0},{14,2},{0,4},{2,6},{4,8},{6,10},{8,12},{10,14},{13,1},{15,3... | collective-permute-start | bytes 884744 | tf_op jit(solution)/shard_map/ppermute | solution.py:177
  13.5 28.9 %all-to-all-start = ((bf16[16,128,256]{2,1,0:T(8,128)(2,1)}), bf16[16,128,256]{2,1,0:T(8,128)(2,1)S(1)}, u32[]{:S(2)}, u32[]{:S(2)}) async-start(bf16[16,128,256]{2,1,0:T(8,128)(2,1)} %pick_prompts.1), calls=%async_computation | async-start | bytes 2097152 | tf_op jit(solution)/shard_map/all_to_all | solution.py:193
  23.2 11.0 %collective-permute-start.4 = (bf16[64,2304]{1,0:T(8,128)(2,1)}, bf16[64,2304]{1,0:T(8,128)(2,1)S(1)}, u32[]{:S(2)}, u32[]{:S(2)}) collective-permute-start(bf16[64,2304]{1,0:T(8,128)(2,1)} %collective-permute-done.2), channel_id=1, source_target_pairs={{2,0},{4,2},{6,4},{8,6},{10,8},{12,10},{14,12},{0,14},{3,1},{5,3},... | collective-permute-start | bytes 884744 | tf_op jit(solution)/shard_map/ppermute | solution.py:177
  30.9 46.3 %copy-start.2 = (s32[16]{0:T(128)S(1)}, s32[16]{0:T(128)}, u32[]{:S(2)}) copy-start(s32[16]{0:T(128)} %order_ref.3) | copy-start | bytes 196
  30.9 46.3 %copy-start.3 = (s32[16]{0:T(128)S(1)}, s32[16]{0:T(128)}, u32[]{:S(2)}) copy-start(s32[16]{0:T(128)} %length_ref.1) | copy-start | bytes 196
  30.9 8.8 %collective-permute-start.5 = (bf16[64,2304]{1,0:T(8,128)(2,1)}, bf16[64,2304]{1,0:T(8,128)(2,1)S(1)}, u32[]{:S(2)}, u32[]{:S(2)}) collective-permute-start(bf16[64,2304]{1,0:T(8,128)(2,1)} %collective-permute-done.3), channel_id=1, source_target_pairs={{14,0},{0,2},{2,4},{4,6},{6,8},{8,10},{10,12},{12,14},{15,1},{1,3}... | collective-permute-start | bytes 884744 | tf_op jit(solution)/shard_map/ppermute | solution.py:177
  34.2 8.2 %collective-permute-start.6 = (bf16[64,2304]{1,0:T(8,128)(2,1)S(1)}, bf16[64,2304]{1,0:T(8,128)(2,1)S(1)}, u32[]{:S(2)}, u32[]{:S(2)}) collective-permute-start(bf16[64,2304]{1,0:T(8,128)(2,1)S(1)} %collective-permute-done.4), channel_id=1, source_target_pairs={{2,0},{4,2},{6,4},{8,6},{10,8},{12,10},{14,12},{0,14},{3,1},{5,3},... | collective-permute-start | bytes 884744 | tf_op jit(solution)/shard_map/ppermute | solution.py:177
  42.4 1.4 %copy-start = (bf16[8,64,2304]{2,1,0:T(8,128)(2,1)}, bf16[8,64,2304]{2,1,0:T(8,128)(2,1)S(1)}, u32[]{:S(2)}) copy-start(bf16[8,64,2304]{2,1,0:T(8,128)(2,1)S(1)} %bitcast_dynamic-update-slice_fusion.refs_0_) | copy-start | bytes 7077892
  43.9 33.3 %all-to-all-start.1 = ((bf16[16,64,512]{2,1,0:T(8,128)(2,1)}), bf16[16,64,512]{2,1,0:T(8,128)(2,1)S(1)}, u32[]{:S(2)}, u32[]{:S(2)}) async-start(bf16[16,64,512]{2,1,0:T(8,128)(2,1)} %bitcast.36), calls=%async_computation.1 | async-start | bytes 2097152 | tf_op jit(solution)/shard_map/all_to_all | solution.py:197
  51.3 60.9 %collective-permute-start.10 = (bf16[8,64,2304]{2,1,0:T(8,128)(2,1)}, bf16[8,64,2304]{2,1,0:T(8,128)(2,1)}, u32[]{:S(2)}, u32[]{:S(2)}) collective-permute-start(bf16[8,64,2304]{2,1,0:T(8,128)(2,1)} %copy-done), channel_id=1, source_target_pairs={{0,64},{64,128},{128,192},{192,0},{1,65},{65,129},{129,193},{193,1... | collective-permute-start | bytes 7077896 | tf_op jit(solution)/shard_map/ppermute | solution.py:184
  52.6 61.9 %collective-permute-start.9 = (bf16[8,64,2304]{2,1,0:T(8,128)(2,1)}, bf16[8,64,2304]{2,1,0:T(8,128)(2,1)}, u32[]{:S(2)}, u32[]{:S(2)}) collective-permute-start(bf16[8,64,2304]{2,1,0:T(8,128)(2,1)} %copy-done), channel_id=1, source_target_pairs={{0,32},{32,0},{1,33},{33,1},{2,34},{34,2},{3,35},{35,3},{4,36},{36... | collective-permute-start | bytes 7077896 | tf_op jit(solution)/shard_map/ppermute | solution.py:183
  53.0 61.5 %collective-permute-start.8 = (bf16[8,64,2304]{2,1,0:T(8,128)(2,1)}, bf16[8,64,2304]{2,1,0:T(8,128)(2,1)}, u32[]{:S(2)}, u32[]{:S(2)}) collective-permute-start(bf16[8,64,2304]{2,1,0:T(8,128)(2,1)} %copy-done), channel_id=1, source_target_pairs={{0,192},{64,0},{128,64},{192,128},{1,193},{65,1},{129,65},{193,129... | collective-permute-start | bytes 7077896 | tf_op jit(solution)/shard_map/ppermute | solution.py:182
  109.8 4.6 %collective-permute-start.7 = (bf16[8,128,256]{2,1,0:T(8,128)(2,1)S(1)}, bf16[8,128,256]{2,1,0:T(8,128)(2,1)S(1)}, u32[]{:S(2)}, u32[]{:S(2)}) collective-permute-start(bf16[8,128,256]{2,1,0:T(8,128)(2,1)S(1)} %all_to_all.15.own_ref), channel_id=1, source_target_pairs={{0,16},{16,0},{1,17},{17,1},{2,18},{18,2},{3,19},{19,3},{4,20},{20... | collective-permute-start | bytes 1572872 | tf_op jit(solution)/shard_map/ppermute | solution.py:207
  114.5 1.7 %copy-start.1 = (bf16[8,64,2304]{2,1,0:T(8,128)(2,1)S(1)}, bf16[8,64,2304]{2,1,0:T(8,128)(2,1)}, u32[]{:S(2)}) copy-start(bf16[8,64,2304]{2,1,0:T(8,128)(2,1)} %copy-done) | copy-start | bytes 7077892
  121.9 13.8 %collective-permute-start.11 = (bf16[128,2304]{1,0:T(8,128)(2,1)S(1)}, bf16[128,2304]{1,0:T(8,128)(2,1)S(1)}, u32[]{:S(2)}, u32[]{:S(2)}) collective-permute-start(bf16[128,2304]{1,0:T(8,128)(2,1)S(1)} %get-tuple-element.13), channel_id=1, source_target_pairs={{0,1},{1,0},{2,3},{3,2},{4,5},{5,4},{6,7},{7,6},{8,9},{9,8},{10,11... | collective-permute-start | bytes 1769480 | tf_op jit(solution)/shard_map/ppermute | solution.py:210
  135.7 5.2 %copy-start.4 = (bf16[1,64,4608]{2,1,0:T(8,128)(2,1)S(1)}, bf16[1,64,4608]{2,1,0:T(8,128)(2,1)}, u32[]{:S(2)}) copy-start(bf16[1,64,4608]{2,1,0:T(8,128)(2,1)} %param.7) | copy-start | bytes 1769476
  135.8 5.2 %copy-start.5 = (f32[4608]{0:T(1024)S(1)}, f32[4608]{0:T(1024)}, u32[]{:S(2)}) copy-start(f32[4608]{0:T(1024)} %param.13) | copy-start | bytes 55300
  135.8 4.9 %collective-permute-start.12 = (bf16[64,2304]{1,0:T(8,128)(2,1)S(1)}, bf16[64,2304]{1,0:T(8,128)(2,1)S(1)}, u32[]{:S(2)}, u32[]{:S(2)}) collective-permute-start(bf16[64,2304]{1,0:T(8,128)(2,1)S(1)} %slice.14), channel_id=1, source_target_pairs={{0,16},{16,0},{1,17},{17,1},{2,18},{18,2},{3,19},{19,3},{4,20},{20... | collective-permute-start | bytes 884744 | tf_op jit(solution)/shard_map/ppermute | solution.py:212

commit v3 on v2

--- a/solution.py
+++ b/solution.py
@@ -15,36 +15,47 @@
 GROUP = ("x", "yl", "core")
 SEQ = ("z", "yh")
 MIB = 1 << 20
-BLOCK_LOTS = ((0, 1, -1, 2, -2, 3, -3, 4),)
-
-
-def pick_kernel(order_ref, src_ref, dst_ref, sems):
-    count = dst_ref.shape[0]
+BLOCK_LOTS = ((0, 1, -1, 2, -2, 3, -3), (4,))
+
+
+def prepare_kernel(order_ref, corner_ref, kv_ref, weight_ref, picked_ref, piece_ref, sems):
+    count = picked_ref.shape[0]
+    rows, cols = piece_ref.shape
+    top = pl.multiple_of(corner_ref[0] * rows, rows)
+    left = pl.multiple_of(corner_ref[1] * cols, cols)
     copies = [
-        pltpu.make_async_copy(src_ref.at[order_ref[i]], dst_ref.at[i], sems.at[i])
-        for i in range(count)
+        pltpu.make_async_copy(
+            weight_ref.at[pl.ds(top, rows), pl.ds(left, cols)], piece_ref, sems.at[count]
+        )
     ]
+    for i in range(count):
+        copies.append(
+            pltpu.make_async_copy(kv_ref.at[order_ref[i]], picked_ref.at[i], sems.at[i])
+        )
     for copy in copies:
         copy.start()
     for copy in copies:
         copy.wait()
 
 
-def pick(order, rows):
+def prepare(order, corner, kv, weight, rows, cols):
+    smem = pl.BlockSpec(memory_space=pltpu.SMEM)
+    vmem = pl.BlockSpec(memory_space=pltpu.VMEM)
+    whole = pl.BlockSpec(memory_space=pltpu.HBM)
     return pl.pallas_call(
-        pick_kernel,
-        out_shape=jax.ShapeDtypeStruct(rows.shape, rows.dtype),
-        in_specs=[
-            pl.BlockSpec(memory_space=pltpu.SMEM),
-            pl.BlockSpec(memory_space=pl.ANY),
-        ],
-        out_specs=pl.BlockSpec(memory_space=pltpu.VMEM),
-        scratch_shapes=[pltpu.SemaphoreType.DMA((rows.shape[0],))],
-        name="pick_prompts",
-    )(order, rows)
-
-
-def attend_kernel(spot_ref, order_ref, length_ref, qkv_ref, kv_ref, out_ref, own_v, prompt_v, *, block):
+        prepare_kernel,
+        out_shape=(
+            jax.ShapeDtypeStruct(kv.shape, kv.dtype),
+            jax.ShapeDtypeStruct((rows, cols), weight.dtype),
+        ),
+        in_specs=[smem, smem, whole, whole],
+        out_specs=(vmem, vmem),
+        scratch_shapes=[pltpu.SemaphoreType.DMA((kv.shape[0] + 1,))],
+        name="prepare",
+    )(order, corner, kv, weight)
+
+
+def attend_kernel(spot_ref, order_ref, length_ref, qkv_ref, kv_ref, out_ref, own_v, prompt_v, *, block, chunk):
     tokens = qkv_ref.shape[0]
     places = kv_ref.shape[0]
     hd = 128
@@ -61,19 +72,27 @@
     cols = lax.broadcasted_iota(jnp.int32, (block, block), 1)
     tri = jnp.where(cols <= rows, 0.0, NEG_FILL).astype(jnp.float32)
     tri = jnp.concatenate([tri, tri], axis=0)
-    for b in range(tokens // block):
+
+    def scores(b):
         at = slice(b * block, (b + 1) * block)
         q = jnp.concatenate([qkv_ref[at, :hd], qkv_ref[at, hd : 2 * hd]], axis=0)
         score = functools.partial(
             lax.dot_general, q, dimension_numbers=dims, preferred_element_type=jnp.float32
         )
-        pieces = [score(kv_ref[:, :hd]) + prompt_bias]
-        values = [prompt_v[...]]
+        pieces, values = [], []
+        for c in range(0, places, chunk):
+            part = slice(c, c + chunk)
+            pieces.append(score(kv_ref[part, :hd]) + prompt_bias[:, part])
+            values.append(prompt_v[part, :])
         if b > 0:
             pieces.append(score(qkv_ref[: b * block, 2 * hd : 3 * hd]))
             values.append(own_v[: b * block, :])
         pieces.append(score(qkv_ref[at, 2 * hd : 3 * hd]) + tri)
         values.append(own_v[at, :])
+        return pieces, values
+
+    def finish(b, pieces, values):
+        at = slice(b * block, (b + 1) * block)
         top = functools.reduce(
             jnp.maximum, [jnp.max(s, axis=-1, keepdims=True) for s in pieces]
         )
@@ -86,12 +105,20 @@
         done = jnp.concatenate([done[:block], done[block:]], axis=1)
         out_ref[at, :] = pltpu.roll(done, spot_ref[1], 1).astype(jnp.bfloat16)
 
-
-def attend(spots, order, lengths, qkv, kv, block=256):
+    count = tokens // block
+    coming = scores(0)
+    for b in range(count):
+        current = coming
+        if b + 1 < count:
+            coming = scores(b + 1)
+        finish(b, *current)
+
+
+def attend(spots, order, lengths, qkv, kv, block=256, chunk=512):
     tokens, places = qkv.shape[0], kv.shape[0]
     vmem = pl.BlockSpec(memory_space=pltpu.VMEM)
     return pl.pallas_call(
-        functools.partial(attend_kernel, block=block),
+        functools.partial(attend_kernel, block=block, chunk=chunk),
         out_shape=jax.ShapeDtypeStruct((tokens, 256), jnp.bfloat16),
         in_specs=[pl.BlockSpec(memory_space=pltpu.SMEM)] * 3 + [vmem, vmem],
         out_specs=vmem,
@@ -170,8 +197,13 @@
     quarter = rows_here // 4
 
     color = (x + 2 * yl) % 4
-    piece = lax.dynamic_slice(
-        out_weight, (color * quarter, core * half_cols), (quarter, half_cols)
+    picked, piece = prepare(
+        cand_prompt,
+        jnp.stack([color, core]).astype(jnp.int32),
+        prompt_kv.reshape(prompt_kv.shape[0], prompt_kv.shape[1], -1),
+        out_weight,
+        quarter,
+        half_cols,
     )
     def from_z(block, distance):
         return lax.ppermute(block, "z", [((i + distance) % nz, i) for i in range(nz)])
@@ -187,26 +219,28 @@
     swap = [(0, 1), (1, 0)]
     blocks = {0: piece, **{d: from_z(piece, d) for d in (1, -1, 2, -2)}}
     blocks.update({3: from_z(blocks[2], 1), -3: from_z(blocks[-2], -1)})
-    blocks[4] = from_z(blocks[3], 1)
-    lots = [jnp.stack([blocks[d] for d in lot]) for lot in BLOCK_LOTS]
-    picked = pick(cand_prompt, prompt_kv.reshape(prompt_kv.shape[0], prompt_kv.shape[1], -1))
+    near = jnp.stack([blocks[d] for d in BLOCK_LOTS[0]])
     prompts = lax.all_to_all(picked, GROUP, 0, 0, tiled=True)
     prompts = prompts.reshape(-1, prompts.shape[-1])
     by_head = cand_qkv[0].transpose(1, 0, 2)
-    by_head, prompts, lots = lax.optimization_barrier((by_head, prompts, lots))
+    by_head, prompts, near = lax.optimization_barrier((by_head, prompts, near))
     qkv = lax.all_to_all(by_head, SEQ, 0, 0, tiled=True).reshape(-1, width)
-    weights = from_sides(lots[0])
+    weights = from_sides(near)
+    qkv, block = lax.optimization_barrier((qkv, blocks[3]))
+    block = from_z(block, 1)
 
     turn = (4 - color) % 4 * quarter
     attended = attend(
         jnp.stack([group, turn]).astype(jnp.int32), cand_prompt, prompt_len, qkv, prompts
     )
+    attended, block = lax.optimization_barrier((attended, block))
     own = lax.all_to_all(
         attended.reshape(nz, -1, attended.shape[-1]), "z", 0, 0, tiled=True
     )
+    own, last = lax.optimization_barrier((own, from_sides(block[None])))
     other = lax.ppermute(own, "core", swap)
     spots = jnp.stack([yh, lax.axis_index("z")]).astype(jnp.int32)
-    send, keep = project(spots, own, other, weights)
+    send, keep = project(spots, own, other, weights + last)
     summed = lax.ppermute(send, "yh", swap).astype(jnp.float32) + keep
     mine, theirs = summed[:per_device], summed[per_device:]
     back = lax.ppermute(theirs.astype(jnp.bfloat16), "core", swap).astype(jnp.float32)

time: 143 us -> 141 us (0.986)
  blocking collectives: 23.2 us -> 0 us
  waiting for transfers between devices: 45.8 us -> 62.1 us
  starting transfers between devices: 41.4 us -> 49.3 us
  local copies, waits for them, and re-layouts: 11.7 us -> 8.83 us
    all_to_all x1 -> x0, blocking collectives: 23.2 us -> none  [body(): lax.all_to_all(attended.reshape(nz, -1, attended.shape[-1]), 'z', 0, 0, t...]
    all_to_all x0 -> x1, starting transfers between devices: none -> 8.37 us  [body(): lax.all_to_all(attended.reshape(nz, -1, attended.shape[-1]), 'z', 0, 0, t...]
    ppermute x1 -> x2, waiting for transfers between devices: 0.01 us -> 8.33 us  [from_sides(): lax.ppermute(lot, 'x', [(i, (i + 1) % nx) for i in range(nx)])]
    ppermute x1 -> x2, waiting for transfers between devices: 2.31 us -> 7.11 us  [from_sides(): lax.ppermute(lot, 'yl', swap)]
    unnamed x20 -> x19, local copies, waits for them, and re-layouts: 11.6 us -> 8.04 us
    ppermute x1, starting transfers between devices: 3.65 us -> 0.97 us  [body(): lax.ppermute(theirs.astype(jnp.bfloat16), 'core', swap).astype(jnp.float32)]
    ppermute x7, starting transfers between devices: 15.5 us -> 13.1 us  [from_z(): lax.ppermute(block, 'z', [((i + distance) % nz, i) for i in range(nz)])]
    ppermute x1, waiting for transfers between devices: 11.2 us -> 13.4 us  [body(): summed = lax.ppermute(send, 'yh', swap).astype(jnp.float32) + keep]
  transfers between devices with their start and end apart: 15 -> 19, of which waited for: 8 -> 9; matrix products, arithmetic and copies ran while one was open for 5% -> 6% of each run, Pallas kernels for 9% -> 6%
where the time goes in v3:
time: 141 us; the launch traced here: 140 us
  waiting for transfers between devices  62.1 us (44%)
  starting transfers between devices  49.3 us (35%)
  Pallas kernels  17.5 us (12%)
  local copies, waits for them, and re-layouts  8.83 us (6%)
  other arithmetic  2.21 us (2%)
    all_to_all x1, waiting for transfers between devices, body(): qkv = lax.all_to_all(by_head, SEQ, 0, 0, tiled=True).reshape(-1, width)  22.8 us
    ppermute x1, waiting for transfers between devices, body(): summed = lax.ppermute(send, 'yh', swap).astype(jnp.float32) + keep  13.4 us
    ppermute x7, starting transfers between devices, from_z(): lax.ppermute(block, 'z', [((i + distance) % nz, i) for i in range(nz)])  13.1 us
    all_to_all x1, starting transfers between devices, body(): lax.all_to_all(attended.reshape(nz, -1, attended.shape[-1]), 'z', 0, 0, t...  8.37 us
    ppermute x2, waiting for transfers between devices, from_sides(): lax.ppermute(lot, 'x', [(i, (i + 1) % nx) for i in range(nx)])  8.33 us
    pallas_call x1, Pallas kernels, attend(): pl.pallas_call(functools.partial(attend_kernel, block=block, chunk=chunk)...  8.32 us
    unnamed x19, local copies, waits for them, and re-layouts  8.04 us
    ppermute x7, waiting for transfers between devices, from_z(): lax.ppermute(block, 'z', [((i + distance) % nz, i) for i in range(nz)])  7.79 us
  transfers between devices with their start and end apart: 19, of which 9 were waited for; matrix products, arithmetic and copies ran while one was open for 6% of the time, Pallas kernels for 6%

profile of v3, /device:TPU:1, one launch (start us, length us, event | category | flops | bytes accessed | tf_op | source)
XLA Modules:
  0.0 140.1 jit_solution(3761808957967745750)
XLA Ops:
  0.0 0.6 pad_add_fusion.2.corner_ref
  0.6 3.2 %prepare.1 = (bf16[16,128,256]{2,1,0:T(8,128)(2,1)}, bf16[64,2304]{1,0:T(8,128)(2,1)}) custom-call(s32[16]{0:T(128)} %order_ref.3, s32[2]{0:T(128)} %pad_add_fusion.2.corner_ref, bf16[16,128,256]{2,1,0:T(8,128)(2,1)} %bitcast.40, bf16[256,4608]{1,0:T(8,128)(2,1)} %weight_ref.1), custom_call_target="tpu_custom_call" | custom-call | tf_op jit(solution)/shard_map/prepare/pallas_call | solution.py:45
  3.8 0.0 copy-start.4
  3.8 0.0 copy-start.2
  3.8 3.9 %collective-permute-start.3 = (bf16[64,2304]{1,0:T(8,128)(2,1)}, bf16[64,2304]{1,0:T(8,128)(2,1)S(1)}, u32[]{:S(2)}, u32[]{:S(2)}) collective-permute-start(bf16[64,2304]{1,0:T(8,128)(2,1)} %get-tuple-element.22), channel_id=1, source_target_pairs={{12,0},{14,2},{0,4},{2,6},{4,8},{6,10},{8,12},{10,14},{13,1},{15,3... | collective-permute-start | bytes 884744 | tf_op jit(solution)/shard_map/ppermute | solution.py:209
  7.7 3.1 %collective-permute-start.2 = (bf16[64,2304]{1,0:T(8,128)(2,1)}, bf16[64,2304]{1,0:T(8,128)(2,1)S(1)}, u32[]{:S(2)}, u32[]{:S(2)}) collective-permute-start(bf16[64,2304]{1,0:T(8,128)(2,1)} %get-tuple-element.22), channel_id=1, source_target_pairs={{4,0},{6,2},{8,4},{10,6},{12,8},{14,10},{0,12},{2,14},{5,1},{7,3},... | collective-permute-start | bytes 884744 | tf_op jit(solution)/shard_map/ppermute | solution.py:209
  10.8 0.7 collective-permute-start.1
  11.6 1.9 %collective-permute-start = (bf16[64,2304]{1,0:T(8,128)(2,1)}, bf16[64,2304]{1,0:T(8,128)(2,1)}, u32[]{:S(2)}, u32[]{:S(2)}) collective-permute-start(bf16[64,2304]{1,0:T(8,128)(2,1)} %get-tuple-element.22), channel_id=1, source_target_pairs={{2,0},{4,2},{6,4},{8,6},{10,8},{12,10},{14,12},{0,14},{3,1},{5,3},... | collective-permute-start | bytes 884744 | tf_op jit(solution)/shard_map/ppermute | solution.py:209
  13.5 6.8 %all-to-all-start = ((bf16[16,128,256]{2,1,0:T(8,128)(2,1)}), bf16[16,128,256]{2,1,0:T(8,128)(2,1)S(1)}, u32[]{:S(2)}, u32[]{:S(2)}) async-start(bf16[16,128,256]{2,1,0:T(8,128)(2,1)} %get-tuple-element.21), calls=%async_computation | async-start | bytes 2097152 | tf_op jit(solution)/shard_map/all_to_all | solution.py:223
  20.3 0.0 copy-done.4
  20.3 0.7 bitcast_dynamic-update-slice_fusion.6
  21.1 0.0 copy-done.2
  21.1 1.7 %copy.11 = bf16[1,64,16,512]{3,1,2,0:T(8,128)(2,1)} copy(bf16[1,64,16,512]{3,2,1,0:T(8,128)(2,1)S(1)} %copy-done.2) | data formatting | bytes 2097152 | tf_op args[1]
  22.7 0.0 collective-permute-done.3
  22.7 2.3 %collective-permute-start.5 = (bf16[64,2304]{1,0:T(8,128)(2,1)S(1)}, bf16[64,2304]{1,0:T(8,128)(2,1)S(1)}, u32[]{:S(2)}, u32[]{:S(2)}) collective-permute-start(bf16[64,2304]{1,0:T(8,128)(2,1)S(1)} %collective-permute-done.3), channel_id=1, source_target_pairs={{14,0},{0,2},{2,4},{4,6},{6,8},{8,10},{10,12},{12,14},{15,1},{1,3}... | collective-permute-start | bytes 884744 | tf_op jit(solution)/shard_map/ppermute | solution.py:209
  25.0 0.5 collective-permute-done.2
  25.6 0.0 collective-permute-start.4
  25.6 5.9 %collective-permute-done = bf16[64,2304]{1,0:T(8,128)(2,1)} collective-permute-done((bf16[64,2304]{1,0:T(8,128)(2,1)}, bf16[64,2304]{1,0:T(8,128)(2,1)}, u32[]{:S(2)}, u32[]{:S(2)}) %collective-permute-start) | collective-permute-done | bytes 294944 | tf_op jit(solution)/shard_map/ppermute | solution.py:209
  31.5 1.7 %bitcast_dynamic-update-slice_fusion.5 = bf16[7,64,2304]{2,1,0:T(8,128)(2,1)} fusion(bf16[7,64,2304]{2,1,0:T(8,128)(2,1)} %bitcast_dynamic-update-slice_fusion.6, bf16[64,2304]{1,0:T(8,128)(2,1)} %collective-permute-done), kind=kLoop, calls=%fused_computation.16 | loop fusion | bytes 589824
  33.2 0.0 collective-permute-done.1
  33.2 1.7 %bitcast_dynamic-update-slice_fusion.4 = bf16[7,64,2304]{2,1,0:T(8,128)(2,1)} fusion(bf16[7,64,2304]{2,1,0:T(8,128)(2,1)} %bitcast_dynamic-update-slice_fusion.5, bf16[64,2304]{1,0:T(8,128)(2,1)} %collective-permute-done.1), kind=kLoop, calls=%fused_computation.15 | loop fusion | bytes 589824
  34.9 0.7 bitcast_dynamic-update-slice_fusion.3
  35.6 0.7 bitcast_dynamic-update-slice_fusion.2
  36.3 1.4 collective-permute-done.4
  37.7 0.8 bitcast_dynamic-update-slice_fusion.1
  38.5 0.0 collective-permute-done.5
  38.5 0.8 bitcast_dynamic-update-slice_fusion.refs_0_
  39.2 0.0 all-to-all-done
  39.2 7.6 %all-to-all-start.1 = ((bf16[16,64,512]{2,1,0:T(8,128)(2,1)}), bf16[16,64,512]{2,1,0:T(8,128)(2,1)S(1)}, u32[]{:S(2)}, u32[]{:S(2)}) async-start(bf16[16,64,512]{2,1,0:T(8,128)(2,1)} %bitcast.31), calls=%async_computation.1 | async-start | bytes 2097152 | tf_op jit(solution)/shard_map/all_to_all | solution.py:227
  46.8 1.3 collective-permute-start.13
  48.1 0.4 collective-permute-start.12
  48.5 1.5 %collective-permute-start.11 = (bf16[7,64,2304]{2,1,0:T(8,128)(2,1)}, bf16[7,64,2304]{2,1,0:T(8,128)(2,1)}, u32[]{:S(2)}, u32[]{:S(2)}) collective-permute-start(bf16[7,64,2304]{2,1,0:T(8,128)(2,1)} %bitcast_dynamic-update-slice_fusion.refs_0_), channel_id=1, source_target_pairs={{0,192},{64,0},{128,64},{192,128},{1,193},{65,1},{129,65},{193,129... | collective-permute-start | bytes 6193160 | tf_op jit(solution)/shard_map/ppermute | solution.py:214
  50.0 22.8 %all-to-all-done.1 = bf16[16,64,512]{2,1,0:T(8,128)(2,1)S(1)} async-done(((bf16[16,64,512]{2,1,0:T(8,128)(2,1)}), bf16[16,64,512]{2,1,0:T(8,128)(2,1)S(1)}, u32[]{:S(2)}, u32[]{:S(2)}) %all-to-all-start.1) | async-done | bytes 1048608 | tf_op jit(solution)/shard_map/all_to_all | solution.py:227
  72.8 1.1 collective-permute-start.6
  73.9 0.1 pad_add_fusion.1.spot_ref
  74.0 0.0 copy-done
  74.0 0.0 copy-done.1
  74.0 8.3 %attend.1 = bf16[1024,256]{1,0:T(8,128)(2,1)} custom-call(s32[2]{0:T(128)S(1)} %pad_add_fusion.1.spot_ref, s32[16]{0:T(128)S(1)} %copy-done, s32[16]{0:T(128)S(1)} %copy-done.1, bf16[1024,512]{1,0:T(8,128)(2,1)S(1)} %bitcast.33, bf16[2048,256]{1,0:T(8,128)(2,1)S(1)} %bitcast.32), custom_call_target="tpu_custom_call" | custom-call | flops 1000000 | bytes 65536 | tf_op jit(solution)/shard_map/attend/pallas_call | solution.py:120
  82.3 0.0 collective-permute-done.6
  82.3 8.4 %all-to-all-start.2 = ((bf16[8,128,256]{2,1,0:T(8,128)(2,1)}), bf16[8,128,256]{2,1,0:T(8,128)(2,1)S(1)}, u32[]{:S(2)}, u32[]{:S(2)}) async-start(bf16[8,128,256]{2,1,0:T(8,128)(2,1)} %bitcast.18), calls=%async_computation.2 | async-start | bytes 1048576 | tf_op jit(solution)/shard_map/all_to_all | solution.py:237
  90.7 1.2 collective-permute-start.9
  91.9 0.4 collective-permute-start.8
  92.3 8.3 %collective-permute-done.9.refs_7_ = bf16[1,64,2304]{2,1,0:T(8,128)(2,1)S(1)} collective-permute-done((bf16[1,64,2304]{2,1,0:T(8,128)(2,1)S(1)}, bf16[1,64,2304]{2,1,0:T(8,128)(2,1)S(1)}, u32[]{:S(2)}, u32[]{:S(2)}) %collective-permute-start.9) | collective-permute-done | bytes 294944 | tf_op jit(solution)/shard_map/ppermute | solution.py:216
  100.6 1.4 collective-permute-start.7
  102.0 7.1 %collective-permute-done.8.refs_6_ = bf16[1,64,2304]{2,1,0:T(8,128)(2,1)S(1)} collective-permute-done((bf16[1,64,2304]{2,1,0:T(8,128)(2,1)S(1)}, bf16[1,64,2304]{2,1,0:T(8,128)(2,1)S(1)}, u32[]{:S(2)}, u32[]{:S(2)}) %collective-permute-start.8) | collective-permute-done | bytes 294944 | tf_op jit(solution)/shard_map/ppermute | solution.py:215
  109.1 0.0 collective-permute-done.7.refs_5_
  109.1 0.0 all-to-all-done.2.own_ref
  109.1 2.8 %collective-permute-start.10 = (bf16[8,128,256]{2,1,0:T(8,128)(2,1)S(1)}, bf16[8,128,256]{2,1,0:T(8,128)(2,1)S(1)}, u32[]{:S(2)}, u32[]{:S(2)}) collective-permute-start(bf16[8,128,256]{2,1,0:T(8,128)(2,1)S(1)} %all-to-all-done.2.own_ref), channel_id=1, source_target_pairs={{0,16},{16,0},{1,17},{17,1},{2,18},{18,2},{3,19},{19,3},{4,20},{20... | collective-permute-start | bytes 1572872 | tf_op jit(solution)/shard_map/ppermute | solution.py:241
  111.9 0.1 pad_add_fusion.spot_ref
  112.0 0.0 collective-permute-done.13.refs_3_
  112.0 0.0 collective-permute-done.12.refs_2_
  112.0 0.0 collective-permute-done.11.refs_1_
  112.0 1.4 %collective-permute-done.10.other_ref = bf16[8,128,256]{2,1,0:T(8,128)(2,1)S(1)} collective-permute-done((bf16[8,128,256]{2,1,0:T(8,128)(2,1)S(1)}, bf16[8,128,256]{2,1,0:T(8,128)(2,1)S(1)}, u32[]{:S(2)}, u32[]{:S(2)}) %collective-permute-start.10) | collective-permute-done | bytes 524320 | tf_op jit(solution)/shard_map/ppermute | solution.py:241
  113.4 6.0 %project.1 = (bf16[128,2304]{1,0:T(8,128)(2,1)S(1)}, f32[128,2304]{1,0:T(8,128)S(1)}) custom-call(s32[2]{0:T(128)S(1)} %pad_add_fusion.spot_ref, bf16[8,128,256]{2,1,0:T(8,128)(2,1)S(1)} %all-to-all-done.2.own_ref, bf16[8,128,256]{2,1,0:T(8,128)(2,1)S(1)} %collective-permute-done.10.other_ref, bf16[7,64,2304]{2,1,0:T(8,128)(2,1)} %bitcast_dynamic-update-slice_fusion.refs_0_, ...), custom_call_target="tpu_custom_call" | custom-call | flops 2415919104 | bytes 12582912 | tf_op jit(solution)/shard_map/project/pallas_call | solution.py:169
  119.5 3.5 %collective-permute-start.14 = (bf16[128,2304]{1,0:T(8,128)(2,1)S(1)}, bf16[128,2304]{1,0:T(8,128)(2,1)S(1)}, u32[]{:S(2)}, u32[]{:S(2)}) collective-permute-start(bf16[128,2304]{1,0:T(8,128)(2,1)S(1)} %get-tuple-element.35), channel_id=1, source_target_pairs={{0,1},{1,0},{2,3},{3,2},{4,5},{5,4},{6,7},{7,6},{8,9},{9,8},{10,11... | collective-permute-start | bytes 1769480 | tf_op jit(solution)/shard_map/ppermute | solution.py:244
  123.0 13.4 %collective-permute-done.14 = bf16[128,2304]{1,0:T(8,128)(2,1)S(1)} collective-permute-done((bf16[128,2304]{1,0:T(8,128)(2,1)S(1)}, bf16[128,2304]{1,0:T(8,128)(2,1)S(1)}, u32[]{:S(2)}, u32[]{:S(2)}) %collective-permute-start.14) | collective-permute-done | bytes 589856 | tf_op jit(solution)/shard_map/ppermute | solution.py:244
  136.4 0.1 convert_add_fusion
  136.5 0.0 copy-start.3
  136.5 0.0 copy-start.5
  136.6 1.0 collective-permute-start.15
  137.6 1.2 collective-permute-done.15
  138.8 0.1 convert_select_fusion.1
  138.9 0.2 fusion.3
  139.1 1.1 fusion.2
  (6 shorter events, 0.0 us)
Async XLA Ops:
  3.8 16.6 %copy-start.4 = (bf16[64,2304]{1,0:T(8,128)(2,1)S(1)}, bf16[64,2304]{1,0:T(8,128)(2,1)}, u32[]{:S(2)}) copy-start(bf16[64,2304]{1,0:T(8,128)(2,1)} %get-tuple-element.22) | copy-start | bytes 884740
  3.8 17.3 %copy-start.2 = (bf16[1,64,16,512]{3,2,1,0:T(8,128)(2,1)S(1)}, bf16[1,64,16,512]{3,2,1,0:T(8,128)(2,1)}, u32[]{:S(2)}) copy-start(bf16[1,64,16,512]{3,2,1,0:T(8,128)(2,1)} %param.8) | copy-start | bytes 3145732
  3.8 18.9 %collective-permute-start.3 = (bf16[64,2304]{1,0:T(8,128)(2,1)}, bf16[64,2304]{1,0:T(8,128)(2,1)S(1)}, u32[]{:S(2)}, u32[]{:S(2)}) collective-permute-start(bf16[64,2304]{1,0:T(8,128)(2,1)} %get-tuple-element.22), channel_id=1, source_target_pairs={{12,0},{14,2},{0,4},{2,6},{4,8},{6,10},{8,12},{10,14},{13,1},{15,3... | collective-permute-start | bytes 884744 | tf_op jit(solution)/shard_map/ppermute | solution.py:209
  7.7 17.9 %collective-permute-start.2 = (bf16[64,2304]{1,0:T(8,128)(2,1)}, bf16[64,2304]{1,0:T(8,128)(2,1)S(1)}, u32[]{:S(2)}, u32[]{:S(2)}) collective-permute-start(bf16[64,2304]{1,0:T(8,128)(2,1)} %get-tuple-element.22), channel_id=1, source_target_pairs={{4,0},{6,2},{8,4},{10,6},{12,8},{14,10},{0,12},{2,14},{5,1},{7,3},... | collective-permute-start | bytes 884744 | tf_op jit(solution)/shard_map/ppermute | solution.py:209
  10.8 22.3 %collective-permute-start.1 = (bf16[64,2304]{1,0:T(8,128)(2,1)}, bf16[64,2304]{1,0:T(8,128)(2,1)}, u32[]{:S(2)}, u32[]{:S(2)}) collective-permute-start(bf16[64,2304]{1,0:T(8,128)(2,1)} %get-tuple-element.22), channel_id=1, source_target_pairs={{14,0},{0,2},{2,4},{4,6},{6,8},{8,10},{10,12},{12,14},{15,1},{1,3}... | collective-permute-start | bytes 884744 | tf_op jit(solution)/shard_map/ppermute | solution.py:209
  11.6 19.9 %collective-permute-start = (bf16[64,2304]{1,0:T(8,128)(2,1)}, bf16[64,2304]{1,0:T(8,128)(2,1)}, u32[]{:S(2)}, u32[]{:S(2)}) collective-permute-start(bf16[64,2304]{1,0:T(8,128)(2,1)} %get-tuple-element.22), channel_id=1, source_target_pairs={{2,0},{4,2},{6,4},{8,6},{10,8},{12,10},{14,12},{0,14},{3,1},{5,3},... | collective-permute-start | bytes 884744 | tf_op jit(solution)/shard_map/ppermute | solution.py:209
  13.5 25.7 %all-to-all-start = ((bf16[16,128,256]{2,1,0:T(8,128)(2,1)}), bf16[16,128,256]{2,1,0:T(8,128)(2,1)S(1)}, u32[]{:S(2)}, u32[]{:S(2)}) async-start(bf16[16,128,256]{2,1,0:T(8,128)(2,1)} %get-tuple-element.21), calls=%async_computation | async-start | bytes 2097152 | tf_op jit(solution)/shard_map/all_to_all | solution.py:223
  22.7 15.7 %collective-permute-start.5 = (bf16[64,2304]{1,0:T(8,128)(2,1)S(1)}, bf16[64,2304]{1,0:T(8,128)(2,1)S(1)}, u32[]{:S(2)}, u32[]{:S(2)}) collective-permute-start(bf16[64,2304]{1,0:T(8,128)(2,1)S(1)} %collective-permute-done.3), channel_id=1, source_target_pairs={{14,0},{0,2},{2,4},{4,6},{6,8},{8,10},{10,12},{12,14},{15,1},{1,3}... | collective-permute-start | bytes 884744 | tf_op jit(solution)/shard_map/ppermute | solution.py:209
  25.6 12.1 %collective-permute-start.4 = (bf16[64,2304]{1,0:T(8,128)(2,1)S(1)}, bf16[64,2304]{1,0:T(8,128)(2,1)S(1)}, u32[]{:S(2)}, u32[]{:S(2)}) collective-permute-start(bf16[64,2304]{1,0:T(8,128)(2,1)S(1)} %collective-permute-done.2), channel_id=1, source_target_pairs={{2,0},{4,2},{6,4},{8,6},{10,8},{12,10},{14,12},{0,14},{3,1},{5,3},... | collective-permute-start | bytes 884744 | tf_op jit(solution)/shard_map/ppermute | solution.py:209
  35.6 38.4 %copy-start = (s32[16]{0:T(128)S(1)}, s32[16]{0:T(128)}, u32[]{:S(2)}) copy-start(s32[16]{0:T(128)} %order_ref.3) | copy-start | bytes 196
  35.6 38.4 %copy-start.1 = (s32[16]{0:T(128)S(1)}, s32[16]{0:T(128)}, u32[]{:S(2)}) copy-start(s32[16]{0:T(128)} %length_ref.1) | copy-start | bytes 196
  39.2 33.6 %all-to-all-start.1 = ((bf16[16,64,512]{2,1,0:T(8,128)(2,1)}), bf16[16,64,512]{2,1,0:T(8,128)(2,1)S(1)}, u32[]{:S(2)}, u32[]{:S(2)}) async-start(bf16[16,64,512]{2,1,0:T(8,128)(2,1)} %bitcast.31), calls=%async_computation.1 | async-start | bytes 2097152 | tf_op jit(solution)/shard_map/all_to_all | solution.py:227
  46.8 65.1 %collective-permute-start.13 = (bf16[7,64,2304]{2,1,0:T(8,128)(2,1)}, bf16[7,64,2304]{2,1,0:T(8,128)(2,1)}, u32[]{:S(2)}, u32[]{:S(2)}) collective-permute-start(bf16[7,64,2304]{2,1,0:T(8,128)(2,1)} %bitcast_dynamic-update-slice_fusion.refs_0_), channel_id=1, source_target_pairs={{0,64},{64,128},{128,192},{192,0},{1,65},{65,129},{129,193},{193,1... | collective-permute-start | bytes 6193160 | tf_op jit(solution)/shard_map/ppermute | solution.py:216
  48.1 63.8 %collective-permute-start.12 = (bf16[7,64,2304]{2,1,0:T(8,128)(2,1)}, bf16[7,64,2304]{2,1,0:T(8,128)(2,1)}, u32[]{:S(2)}, u32[]{:S(2)}) collective-permute-start(bf16[7,64,2304]{2,1,0:T(8,128)(2,1)} %bitcast_dynamic-update-slice_fusion.refs_0_), channel_id=1, source_target_pairs={{0,32},{32,0},{1,33},{33,1},{2,34},{34,2},{3,35},{35,3},{4,36},{36... | collective-permute-start | bytes 6193160 | tf_op jit(solution)/shard_map/ppermute | solution.py:215
  48.5 63.4 %collective-permute-start.11 = (bf16[7,64,2304]{2,1,0:T(8,128)(2,1)}, bf16[7,64,2304]{2,1,0:T(8,128)(2,1)}, u32[]{:S(2)}, u32[]{:S(2)}) collective-permute-start(bf16[7,64,2304]{2,1,0:T(8,128)(2,1)} %bitcast_dynamic-update-slice_fusion.refs_0_), channel_id=1, source_target_pairs={{0,192},{64,0},{128,64},{192,128},{1,193},{65,1},{129,65},{193,129... | collective-permute-start | bytes 6193160 | tf_op jit(solution)/shard_map/ppermute | solution.py:214
  72.8 9.5 %collective-permute-start.6 = (bf16[64,2304]{1,0:T(8,128)(2,1)S(1)}, bf16[64,2304]{1,0:T(8,128)(2,1)S(1)}, u32[]{:S(2)}, u32[]{:S(2)}) collective-permute-start(bf16[64,2304]{1,0:T(8,128)(2,1)S(1)} %collective-permute-done.4), channel_id=1, source_target_pairs={{2,0},{4,2},{6,4},{8,6},{10,8},{12,10},{14,12},{0,14},{3,1},{5,3},... | collective-permute-start | bytes 884744 | tf_op jit(solution)/shard_map/ppermute | solution.py:209
  82.3 26.8 %all-to-all-start.2 = ((bf16[8,128,256]{2,1,0:T(8,128)(2,1)}), bf16[8,128,256]{2,1,0:T(8,128)(2,1)S(1)}, u32[]{:S(2)}, u32[]{:S(2)}) async-start(bf16[8,128,256]{2,1,0:T(8,128)(2,1)} %bitcast.18), calls=%async_computation.2 | async-start | bytes 1048576 | tf_op jit(solution)/shard_map/all_to_all | solution.py:237
  90.7 9.9 %collective-permute-start.9 = (bf16[1,64,2304]{2,1,0:T(8,128)(2,1)S(1)}, bf16[1,64,2304]{2,1,0:T(8,128)(2,1)S(1)}, u32[]{:S(2)}, u32[]{:S(2)}) collective-permute-start(bf16[1,64,2304]{2,1,0:T(8,128)(2,1)S(1)} %bitcast.34), channel_id=1, source_target_pairs={{0,64},{64,128},{128,192},{192,0},{1,65},{65,129},{129,193},{193,1... | collective-permute-start | bytes 884744 | tf_op jit(solution)/shard_map/ppermute | solution.py:216
  91.9 17.2 %collective-permute-start.8 = (bf16[1,64,2304]{2,1,0:T(8,128)(2,1)S(1)}, bf16[1,64,2304]{2,1,0:T(8,128)(2,1)S(1)}, u32[]{:S(2)}, u32[]{:S(2)}) collective-permute-start(bf16[1,64,2304]{2,1,0:T(8,128)(2,1)S(1)} %bitcast.35), channel_id=1, source_target_pairs={{0,32},{32,0},{1,33},{33,1},{2,34},{34,2},{3,35},{35,3},{4,36},{36... | collective-permute-start | bytes 884744 | tf_op jit(solution)/shard_map/ppermute | solution.py:215
  100.6 8.5 %collective-permute-start.7 = (bf16[1,64,2304]{2,1,0:T(8,128)(2,1)S(1)}, bf16[1,64,2304]{2,1,0:T(8,128)(2,1)S(1)}, u32[]{:S(2)}, u32[]{:S(2)}) collective-permute-start(bf16[1,64,2304]{2,1,0:T(8,128)(2,1)S(1)} %bitcast.36), channel_id=1, source_target_pairs={{0,192},{64,0},{128,64},{192,128},{1,193},{65,1},{129,65},{193,129... | collective-permute-start | bytes 884744 | tf_op jit(solution)/shard_map/ppermute | solution.py:214
  109.1 4.3 %collective-permute-start.10 = (bf16[8,128,256]{2,1,0:T(8,128)(2,1)S(1)}, bf16[8,128,256]{2,1,0:T(8,128)(2,1)S(1)}, u32[]{:S(2)}, u32[]{:S(2)}) collective-permute-start(bf16[8,128,256]{2,1,0:T(8,128)(2,1)S(1)} %all-to-all-done.2.own_ref), channel_id=1, source_target_pairs={{0,16},{16,0},{1,17},{17,1},{2,18},{18,2},{3,19},{19,3},{4,20},{20... | collective-permute-start | bytes 1572872 | tf_op jit(solution)/shard_map/ppermute | solution.py:241
  119.5 16.9 %collective-permute-start.14 = (bf16[128,2304]{1,0:T(8,128)(2,1)S(1)}, bf16[128,2304]{1,0:T(8,128)(2,1)S(1)}, u32[]{:S(2)}, u32[]{:S(2)}) collective-permute-start(bf16[128,2304]{1,0:T(8,128)(2,1)S(1)} %get-tuple-element.35), channel_id=1, source_target_pairs={{0,1},{1,0},{2,3},{3,2},{4,5},{5,4},{6,7},{7,6},{8,9},{9,8},{10,11... | collective-permute-start | bytes 1769480 | tf_op jit(solution)/shard_map/ppermute | solution.py:244
  136.5 2.5 %copy-start.3 = (bf16[1,64,4608]{2,1,0:T(8,128)(2,1)S(1)}, bf16[1,64,4608]{2,1,0:T(8,128)(2,1)}, u32[]{:S(2)}) copy-start(bf16[1,64,4608]{2,1,0:T(8,128)(2,1)} %param.7) | copy-start | bytes 1769476
  136.5 2.5 %copy-start.5 = (f32[4608]{0:T(1024)S(1)}, f32[4608]{0:T(1024)}, u32[]{:S(2)}) copy-start(f32[4608]{0:T(1024)} %param.13) | copy-start | bytes 55300
  136.6 2.2 %collective-permute-start.15 = (bf16[64,2304]{1,0:T(8,128)(2,1)S(1)}, bf16[64,2304]{1,0:T(8,128)(2,1)S(1)}, u32[]{:S(2)}, u32[]{:S(2)}) collective-permute-start(bf16[64,2304]{1,0:T(8,128)(2,1)S(1)} %slice.14), channel_id=1, source_target_pairs={{0,16},{16,0},{1,17},{17,1},{2,18},{18,2},{3,19},{19,3},{4,20},{20... | collective-permute-start | bytes 884744 | tf_op jit(solution)/shard_map/ppermute | solution.py:246

commit v4 on v3

--- a/solution.py
+++ b/solution.py
@@ -15,14 +15,15 @@
 GROUP = ("x", "yl", "core")
 SEQ = ("z", "yh")
 MIB = 1 << 20
-BLOCK_LOTS = ((0, 1, -1, 2, -2, 3, -3), (4,))
-
-
-def prepare_kernel(order_ref, corner_ref, kv_ref, weight_ref, picked_ref, piece_ref, sems):
+BLOCK_LOTS = ((1, -1, 2, -2, 3, -3), (4,))
+
+
+def prepare_kernel(order_ref, kv_ref, weight_ref, picked_ref, piece_ref, sems):
     count = picked_ref.shape[0]
     rows, cols = piece_ref.shape
-    top = pl.multiple_of(corner_ref[0] * rows, rows)
-    left = pl.multiple_of(corner_ref[1] * cols, cols)
+    color = (lax.axis_index("x") + 2 * lax.axis_index("yl")) % 4
+    top = pl.multiple_of(color * rows, rows)
+    left = pl.multiple_of(lax.axis_index("core") * cols, cols)
     copies = [
         pltpu.make_async_copy(
             weight_ref.at[pl.ds(top, rows), pl.ds(left, cols)], piece_ref, sems.at[count]
@@ -38,7 +39,7 @@
         copy.wait()
 
 
-def prepare(order, corner, kv, weight, rows, cols):
+def prepare(order, kv, weight, rows, cols):
     smem = pl.BlockSpec(memory_space=pltpu.SMEM)
     vmem = pl.BlockSpec(memory_space=pltpu.VMEM)
     whole = pl.BlockSpec(memory_space=pltpu.HBM)
@@ -48,11 +49,11 @@
             jax.ShapeDtypeStruct(kv.shape, kv.dtype),
             jax.ShapeDtypeStruct((rows, cols), weight.dtype),
         ),
-        in_specs=[smem, smem, whole, whole],
+        in_specs=[smem, whole, whole],
         out_specs=(vmem, vmem),
         scratch_shapes=[pltpu.SemaphoreType.DMA((kv.shape[0] + 1,))],
         name="prepare",
-    )(order, corner, kv, weight)
+    )(order, kv, weight)
 
 
 def attend_kernel(spot_ref, order_ref, length_ref, qkv_ref, kv_ref, out_ref, own_v, prompt_v, *, block, chunk):
@@ -134,25 +135,35 @@
     )(spots, order, lengths, qkv, kv)
 
 
-def project_kernel(spot_ref, own_ref, other_ref, *refs):
+def project_kernel(spot_ref, own_ref, other_ref, local, *refs):
     weights, (send_ref, keep_ref, total) = refs[:-3], refs[-3:]
     blocks = own_ref.shape[0]
-    cols = keep_ref.shape[1]
+    rows, cols = local.shape
+    quarter = rows // 4
     half = own_ref.shape[1] // 2
     here = pl.multiple_of(spot_ref[0] * half, half)
     there = pl.multiple_of((1 - spot_ref[0]) * half, half)
     width = 256
-    places = [(lot, k) for lot in range(len(weights) // 4) for k in range(weights[4 * lot].shape[0])]
-    for r, (lot, k) in enumerate(places):
-        n = lax.rem(spot_ref[1] + BLOCK_LOTS[lot][k] + blocks, blocks)
+    places = [(d, lot, k) for lot, distances in enumerate(BLOCK_LOTS) for k, d in enumerate(distances)]
+    places.append((0, None, None))
+    for r, (distance, lot, k) in enumerate(places):
+        n = lax.rem(spot_ref[1] + distance + blocks, blocks)
         tokens = jnp.concatenate(
             [ref[n, pl.ds(at, half), :] for at in (there, here) for ref in (own_ref, other_ref)],
             axis=0,
         )
         for j in range(cols // width):
             at = slice(j * width, (j + 1) * width)
-            block = jnp.concatenate([weights[4 * lot + i][k, :, at] for i in range(4)], axis=0)
-            part = jnp.dot(tokens, block, preferred_element_type=jnp.float32)
+            if lot is None:
+                quarters = []
+                for i in range(4):
+                    top = pl.multiple_of(lax.rem(spot_ref[2] + i, 4) * quarter, quarter)
+                    quarters.append(local[pl.ds(top, quarter), at])
+            else:
+                quarters = [weights[4 * lot + i][k, :, at] for i in range(4)]
+            part = jnp.dot(
+                tokens, jnp.concatenate(quarters, axis=0), preferred_element_type=jnp.float32
+            )
             if r > 0:
                 part = part + total[:, at]
             if r < blocks - 1:
@@ -162,7 +173,7 @@
                 keep_ref[:, at] = part[2 * half :]
 
 
-def project(spots, own, other, weights):
+def project(spots, own, other, local, weights):
     vmem = pl.BlockSpec(memory_space=pltpu.VMEM)
     quarter, cols = weights[0].shape[1:]
     blocks, tokens = own.shape[:2]
@@ -172,9 +183,11 @@
             jax.ShapeDtypeStruct((tokens, cols), jnp.bfloat16),
             jax.ShapeDtypeStruct((tokens, cols), jnp.float32),
         ),
-        in_specs=[pl.BlockSpec(memory_space=pltpu.SMEM)] + [vmem] * (2 + len(weights)),
+        in_specs=[pl.BlockSpec(memory_space=pltpu.SMEM)] + [vmem] * (3 + len(weights)),
         out_specs=(vmem, vmem),
-        scratch_shapes=[pltpu.VMEM((2 * tokens, cols), jnp.float32)],
+        scratch_shapes=[
+            pltpu.VMEM((2 * tokens, cols), jnp.float32),
+        ],
         compiler_params=pltpu.CompilerParams(vmem_limit_bytes=32 * MIB),
         cost_estimate=pl.CostEstimate(
             flops=2 * 2 * tokens * blocks * 4 * quarter * cols,
@@ -182,7 +195,7 @@
             transcendentals=0,
         ),
         name="project",
-    )(spots, own, other, *weights)
+    )(spots, own, other, local, *weights)
 
 
 def body(residual, cand_qkv, prompt_kv, prompt_len, cand_prompt, out_weight, post_gain):
@@ -199,7 +212,6 @@
     color = (x + 2 * yl) % 4
     picked, piece = prepare(
         cand_prompt,
-        jnp.stack([color, core]).astype(jnp.int32),
         prompt_kv.reshape(prompt_kv.shape[0], prompt_kv.shape[1], -1),
         out_weight,
         quarter,
@@ -234,13 +246,15 @@
         jnp.stack([group, turn]).astype(jnp.int32), cand_prompt, prompt_len, qkv, prompts
     )
     attended, block = lax.optimization_barrier((attended, block))
+    block, weights[1], weights[3] = lax.optimization_barrier((block, weights[1], weights[3]))
     own = lax.all_to_all(
         attended.reshape(nz, -1, attended.shape[-1]), "z", 0, 0, tiled=True
     )
     own, last = lax.optimization_barrier((own, from_sides(block[None])))
     other = lax.ppermute(own, "core", swap)
-    spots = jnp.stack([yh, lax.axis_index("z")]).astype(jnp.int32)
-    send, keep = project(spots, own, other, weights + last)
+    spots = jnp.stack([yh, lax.axis_index("z"), color]).astype(jnp.int32)
+    local = lax.dynamic_slice(out_weight, (0, core * half_cols), (rows_here, half_cols))
+    send, keep = project(spots, own, other, local, weights + last)
     summed = lax.ppermute(send, "yh", swap).astype(jnp.float32) + keep
     mine, theirs = summed[:per_device], summed[per_device:]
     back = lax.ppermute(theirs.astype(jnp.bfloat16), "core", swap).astype(jnp.float32)

time: 141 us -> 136 us (0.965)
  starting transfers between devices: 49.3 us -> 45.6 us
    all_to_all x1, waiting for transfers between devices: 0.01 us -> 4.64 us  [body(): lax.all_to_all(attended.reshape(nz, -1, attended.shape[-1]), 'z', 0, 0, t...]
    ppermute x1, starting transfers between devices: 3.55 us -> 0.72 us  [body(): summed = lax.ppermute(send, 'yh', swap).astype(jnp.float32) + keep]
    ppermute x2, waiting for transfers between devices: 8.33 us -> 5.53 us  [from_sides(): lax.ppermute(lot, 'x', [(i, (i + 1) % nx) for i in range(nx)])]
    ppermute x2, waiting for transfers between devices: 7.11 us -> 4.53 us  [from_sides(): lax.ppermute(lot, 'yl', swap)]
    ppermute x1, starting transfers between devices: 2.75 us -> 0.58 us  [body(): other = lax.ppermute(own, 'core', swap)]
    ppermute x1, waiting for transfers between devices: 13.4 us -> 15.4 us  [body(): summed = lax.ppermute(send, 'yh', swap).astype(jnp.float32) + keep]
    unnamed x19 -> x16, local copies, waits for them, and re-layouts: 8.04 us -> 6.3 us
  transfers between devices with their start and end apart: 19 -> 19, of which waited for: 9 -> 10; matrix products, arithmetic and copies ran while one was open for 6% -> 6% of each run, Pallas kernels for 6% -> 6%
where the time goes in v4:
time: 136 us
  waiting for transfers between devices  63 us (46%)
  starting transfers between devices  45.6 us (34%)
  Pallas kernels  17.2 us (13%)
  local copies, waits for them, and re-layouts  8.42 us (6%)
  other arithmetic  1.6 us (1%)
    all_to_all x1, waiting for transfers between devices, body(): qkv = lax.all_to_all(by_head, SEQ, 0, 0, tiled=True).reshape(-1, width)  22.8 us
    ppermute x1, waiting for transfers between devices, body(): summed = lax.ppermute(send, 'yh', swap).astype(jnp.float32) + keep  15.4 us
    ppermute x7, starting transfers between devices, from_z(): lax.ppermute(block, 'z', [((i + distance) % nz, i) for i in range(nz)])  13.9 us
    ppermute x7, waiting for transfers between devices, from_z(): lax.ppermute(block, 'z', [((i + distance) % nz, i) for i in range(nz)])  8.71 us
    all_to_all x1, starting transfers between devices, body(): lax.all_to_all(attended.reshape(nz, -1, attended.shape[-1]), 'z', 0, 0, t...  8.36 us
    pallas_call x1, Pallas kernels, attend(): pl.pallas_call(functools.partial(attend_kernel, block=block, chunk=chunk)...  8.32 us
    all_to_all x1, starting transfers between devices, body(): qkv = lax.all_to_all(by_head, SEQ, 0, 0, tiled=True).reshape(-1, width)  7.62 us
    all_to_all x1, starting transfers between devices, body(): prompts = lax.all_to_all(picked, GROUP, 0, 0, tiled=True)  6.84 us
  transfers between devices with their start and end apart: 19, of which 10 were waited for; matrix products, arithmetic and copies ran while one was open for 6% of the time, Pallas kernels for 6%

profile of v4, /device:TPU:1, one launch (start us, length us, event | category | flops | bytes accessed | tf_op | source)
XLA Modules:
  0.0 135.9 jit_solution(1269877046988139804)
XLA Ops:
  0.0 3.2 %prepare.1 = (bf16[16,128,256]{2,1,0:T(8,128)(2,1)}, bf16[64,2304]{1,0:T(8,128)(2,1)}) custom-call(s32[16]{0:T(128)} %order_ref.3, bf16[16,128,256]{2,1,0:T(8,128)(2,1)} %bitcast.37, bf16[256,4608]{1,0:T(8,128)(2,1)} %weight_ref.1), custom_call_target="tpu_custom_call" | custom-call | tf_op jit(solution)/shard_map/prepare/pallas_call | solution.py:46
  3.2 0.0 copy-start.2
  3.2 3.9 %collective-permute-start.3 = (bf16[64,2304]{1,0:T(8,128)(2,1)}, bf16[64,2304]{1,0:T(8,128)(2,1)S(1)}, u32[]{:S(2)}, u32[]{:S(2)}) collective-permute-start(bf16[64,2304]{1,0:T(8,128)(2,1)} %get-tuple-element.25), channel_id=1, source_target_pairs={{12,0},{14,2},{0,4},{2,6},{4,8},{6,10},{8,12},{10,14},{13,1},{15,3... | collective-permute-start | bytes 884744 | tf_op jit(solution)/shard_map/ppermute | solution.py:221
  7.1 3.1 %collective-permute-start.2 = (bf16[64,2304]{1,0:T(8,128)(2,1)}, bf16[64,2304]{1,0:T(8,128)(2,1)S(1)}, u32[]{:S(2)}, u32[]{:S(2)}) collective-permute-start(bf16[64,2304]{1,0:T(8,128)(2,1)} %get-tuple-element.25), channel_id=1, source_target_pairs={{4,0},{6,2},{8,4},{10,6},{12,8},{14,10},{0,12},{2,14},{5,1},{7,3},... | collective-permute-start | bytes 884744 | tf_op jit(solution)/shard_map/ppermute | solution.py:221
  10.2 1.8 %collective-permute-start = (bf16[64,2304]{1,0:T(8,128)(2,1)}, bf16[64,2304]{1,0:T(8,128)(2,1)}, u32[]{:S(2)}, u32[]{:S(2)}) collective-permute-start(bf16[64,2304]{1,0:T(8,128)(2,1)} %get-tuple-element.25), channel_id=1, source_target_pairs={{2,0},{4,2},{6,4},{8,6},{10,8},{12,10},{14,12},{0,14},{3,1},{5,3},... | collective-permute-start | bytes 884744 | tf_op jit(solution)/shard_map/ppermute | solution.py:221
  12.0 0.0 collective-permute-start.1
  12.0 6.8 %all-to-all-start = ((bf16[16,128,256]{2,1,0:T(8,128)(2,1)}), bf16[16,128,256]{2,1,0:T(8,128)(2,1)S(1)}, u32[]{:S(2)}, u32[]{:S(2)}) async-start(bf16[16,128,256]{2,1,0:T(8,128)(2,1)} %get-tuple-element.24), calls=%async_computation | async-start | bytes 2097152 | tf_op jit(solution)/shard_map/all_to_all | solution.py:235
  18.9 0.0 copy-done.2
  18.9 1.6 %copy.11 = bf16[1,64,16,512]{3,1,2,0:T(8,128)(2,1)} copy(bf16[1,64,16,512]{3,2,1,0:T(8,128)(2,1)S(1)} %copy-done.2) | data formatting | bytes 2097152 | tf_op args[1]
  20.5 0.0 collective-permute-done.3
  20.5 3.9 %collective-permute-start.5 = (bf16[64,2304]{1,0:T(8,128)(2,1)S(1)}, bf16[64,2304]{1,0:T(8,128)(2,1)S(1)}, u32[]{:S(2)}, u32[]{:S(2)}) collective-permute-start(bf16[64,2304]{1,0:T(8,128)(2,1)S(1)} %collective-permute-done.3), channel_id=1, source_target_pairs={{14,0},{0,2},{2,4},{4,6},{6,8},{8,10},{10,12},{12,14},{15,1},{1,3}... | collective-permute-start | bytes 884744 | tf_op jit(solution)/shard_map/ppermute | solution.py:221
  24.4 0.4 collective-permute-done.2
  24.8 0.0 collective-permute-start.4
  24.8 6.0 %collective-permute-done = bf16[64,2304]{1,0:T(8,128)(2,1)} collective-permute-done((bf16[64,2304]{1,0:T(8,128)(2,1)}, bf16[64,2304]{1,0:T(8,128)(2,1)}, u32[]{:S(2)}, u32[]{:S(2)}) %collective-permute-start) | collective-permute-done | bytes 294944 | tf_op jit(solution)/shard_map/ppermute | solution.py:221
  30.9 1.7 %bitcast_dynamic-update-slice_fusion.5 = bf16[6,64,2304]{2,1,0:T(8,128)(2,1)} fusion(bf16[64,2304]{1,0:T(8,128)(2,1)} %collective-permute-done), kind=kLoop, calls=%fused_computation.16 | loop fusion | bytes 589824
  32.6 0.0 collective-permute-done.1
  32.6 0.7 bitcast_dynamic-update-slice_fusion.4
  33.3 0.7 bitcast_dynamic-update-slice_fusion.3
  34.0 0.7 bitcast_dynamic-update-slice_fusion.2
  34.8 0.0 copy-start
  34.8 2.3 %collective-permute-done.4 = bf16[64,2304]{1,0:T(8,128)(2,1)S(1)} collective-permute-done((bf16[64,2304]{1,0:T(8,128)(2,1)S(1)}, bf16[64,2304]{1,0:T(8,128)(2,1)S(1)}, u32[]{:S(2)}, u32[]{:S(2)}) %collective-permute-start.4) | collective-permute-done | bytes 294944 | tf_op jit(solution)/shard_map/ppermute | solution.py:221
  37.1 0.7 bitcast_dynamic-update-slice_fusion.1
  37.8 0.0 collective-permute-done.5
  37.8 0.7 bitcast_dynamic-update-slice_fusion.refs_0_
  38.6 0.0 all-to-all-done
  38.6 7.6 %all-to-all-start.1 = ((bf16[16,64,512]{2,1,0:T(8,128)(2,1)}), bf16[16,64,512]{2,1,0:T(8,128)(2,1)S(1)}, u32[]{:S(2)}, u32[]{:S(2)}) async-start(bf16[16,64,512]{2,1,0:T(8,128)(2,1)} %bitcast.28), calls=%async_computation.1 | async-start | bytes 2097152 | tf_op jit(solution)/shard_map/all_to_all | solution.py:239
  46.2 1.3 collective-permute-start.8
  47.5 1.5 %collective-permute-start.7 = (bf16[6,64,2304]{2,1,0:T(8,128)(2,1)}, bf16[6,64,2304]{2,1,0:T(8,128)(2,1)}, u32[]{:S(2)}, u32[]{:S(2)}) collective-permute-start(bf16[6,64,2304]{2,1,0:T(8,128)(2,1)} %bitcast_dynamic-update-slice_fusion.refs_0_), channel_id=1, source_target_pairs={{0,192},{64,0},{128,64},{192,128},{1,193},{65,1},{129,65},{193,129... | collective-permute-start | bytes 5308424 | tf_op jit(solution)/shard_map/ppermute | solution.py:226
  48.9 0.4 collective-permute-start.13
  49.3 22.8 %all-to-all-done.1 = bf16[16,64,512]{2,1,0:T(8,128)(2,1)S(1)} async-done(((bf16[16,64,512]{2,1,0:T(8,128)(2,1)}), bf16[16,64,512]{2,1,0:T(8,128)(2,1)S(1)}, u32[]{:S(2)}, u32[]{:S(2)}) %all-to-all-start.1) | async-done | bytes 1048608 | tf_op jit(solution)/shard_map/all_to_all | solution.py:239
  72.2 1.1 collective-permute-start.6
  73.3 0.1 pad_add_fusion.1.spot_ref
  73.4 0.0 copy-done
  73.4 0.0 copy-done.1
  73.4 8.3 %attend.1 = bf16[1024,256]{1,0:T(8,128)(2,1)} custom-call(s32[2]{0:T(128)S(1)} %pad_add_fusion.1.spot_ref, s32[16]{0:T(128)S(1)} %copy-done, s32[16]{0:T(128)S(1)} %copy-done.1, bf16[1024,512]{1,0:T(8,128)(2,1)S(1)} %bitcast.30, bf16[2048,256]{1,0:T(8,128)(2,1)S(1)} %bitcast.29), custom_call_target="tpu_custom_call" | custom-call | flops 1000000 | bytes 65536 | tf_op jit(solution)/shard_map/attend/pallas_call | solution.py:121
  81.7 0.0 collective-permute-done.6
  81.7 8.4 %all-to-all-start.2 = ((bf16[8,128,256]{2,1,0:T(8,128)(2,1)}), bf16[8,128,256]{2,1,0:T(8,128)(2,1)S(1)}, u32[]{:S(2)}, u32[]{:S(2)}) async-start(bf16[8,128,256]{2,1,0:T(8,128)(2,1)} %bitcast.16), calls=%async_computation.2 | async-start | bytes 1048576 | tf_op jit(solution)/shard_map/all_to_all | solution.py:250
  90.0 0.0 collective-permute-done.8.refs_3_
  90.1 0.0 collective-permute-done.7.refs_1_
  90.1 1.3 collective-permute-start.11
  91.4 0.4 collective-permute-start.10
  91.8 1.5 %collective-permute-start.9 = (bf16[1,64,2304]{2,1,0:T(8,128)(2,1)S(1)}, bf16[1,64,2304]{2,1,0:T(8,128)(2,1)S(1)}, u32[]{:S(2)}, u32[]{:S(2)}) collective-permute-start(bf16[1,64,2304]{2,1,0:T(8,128)(2,1)S(1)} %bitcast.33), channel_id=1, source_target_pairs={{0,192},{64,0},{128,64},{192,128},{1,193},{65,1},{129,65},{193,129... | collective-permute-start | bytes 884744 | tf_op jit(solution)/shard_map/ppermute | solution.py:226
  93.2 5.5 %collective-permute-done.11.refs_7_ = bf16[1,64,2304]{2,1,0:T(8,128)(2,1)S(1)} collective-permute-done((bf16[1,64,2304]{2,1,0:T(8,128)(2,1)S(1)}, bf16[1,64,2304]{2,1,0:T(8,128)(2,1)S(1)}, u32[]{:S(2)}, u32[]{:S(2)}) %collective-permute-start.11) | collective-permute-done | bytes 294944 | tf_op jit(solution)/shard_map/ppermute | solution.py:228
  98.7 4.5 %collective-permute-done.10.refs_6_ = bf16[1,64,2304]{2,1,0:T(8,128)(2,1)S(1)} collective-permute-done((bf16[1,64,2304]{2,1,0:T(8,128)(2,1)S(1)}, bf16[1,64,2304]{2,1,0:T(8,128)(2,1)S(1)}, u32[]{:S(2)}, u32[]{:S(2)}) %collective-permute-start.10) | collective-permute-done | bytes 294944 | tf_op jit(solution)/shard_map/ppermute | solution.py:227
  103.3 0.0 collective-permute-done.9.refs_5_
  103.3 4.6 %all-to-all-done.2.own_ref = bf16[8,128,256]{2,1,0:T(8,128)(2,1)S(1)} async-done(((bf16[8,128,256]{2,1,0:T(8,128)(2,1)}), bf16[8,128,256]{2,1,0:T(8,128)(2,1)S(1)}, u32[]{:S(2)}, u32[]{:S(2)}) %all-to-all-start.2) | async-done | bytes 524320 | tf_op jit(solution)/shard_map/all_to_all | solution.py:250
  107.9 0.6 collective-permute-start.12
  108.5 0.1 pad_add_fusion.spot_ref
  108.6 1.3 constant_dynamic-slice_fusion.local
  109.9 0.0 collective-permute-done.13.refs_2_
  109.9 0.1 collective-permute-done.12.other_ref
  110.0 5.7 %project.1 = (bf16[128,2304]{1,0:T(8,128)(2,1)S(1)}, f32[128,2304]{1,0:T(8,128)S(1)}) custom-call(s32[3]{0:T(128)S(1)} %pad_add_fusion.spot_ref, bf16[8,128,256]{2,1,0:T(8,128)(2,1)S(1)} %all-to-all-done.2.own_ref, bf16[8,128,256]{2,1,0:T(8,128)(2,1)S(1)} %collective-permute-done.12.other_ref, bf16[256,2304]{1,0:T(8,128)(2,1)S(1)} %constant_dynamic-slice_fusion.local, ...), custom_call_target="tpu_custom_call" | custom-call | flops 2415919104 | bytes 12582912 | tf_op jit(solution)/shard_map/project/pallas_call | solution.py:180
  115.7 0.7 collective-permute-start.14
  116.5 15.4 %collective-permute-done.14 = bf16[128,2304]{1,0:T(8,128)(2,1)S(1)} collective-permute-done((bf16[128,2304]{1,0:T(8,128)(2,1)S(1)}, bf16[128,2304]{1,0:T(8,128)(2,1)S(1)}, u32[]{:S(2)}, u32[]{:S(2)}) %collective-permute-start.14) | collective-permute-done | bytes 589856 | tf_op jit(solution)/shard_map/ppermute | solution.py:258
  131.9 0.1 convert_add_fusion
  132.0 0.0 copy-start.3
  132.0 0.0 copy-start.4
  132.0 1.3 collective-permute-start.15
  133.3 1.2 collective-permute-done.15
  134.5 0.1 convert_select_fusion.1
  134.6 0.2 fusion.3
  134.8 0.0 copy-done.3
  134.8 0.0 copy-done.4
  134.8 1.1 fusion.2
  (3 shorter events, 0.0 us)
Async XLA Ops:
  3.2 15.7 %copy-start.2 = (bf16[1,64,16,512]{3,2,1,0:T(8,128)(2,1)S(1)}, bf16[1,64,16,512]{3,2,1,0:T(8,128)(2,1)}, u32[]{:S(2)}) copy-start(bf16[1,64,16,512]{3,2,1,0:T(8,128)(2,1)} %param.8) | copy-start | bytes 3145732
  3.2 17.3 %collective-permute-start.3 = (bf16[64,2304]{1,0:T(8,128)(2,1)}, bf16[64,2304]{1,0:T(8,128)(2,1)S(1)}, u32[]{:S(2)}, u32[]{:S(2)}) collective-permute-start(bf16[64,2304]{1,0:T(8,128)(2,1)} %get-tuple-element.25), channel_id=1, source_target_pairs={{12,0},{14,2},{0,4},{2,6},{4,8},{6,10},{8,12},{10,14},{13,1},{15,3... | collective-permute-start | bytes 884744 | tf_op jit(solution)/shard_map/ppermute | solution.py:221
  7.1 17.8 %collective-permute-start.2 = (bf16[64,2304]{1,0:T(8,128)(2,1)}, bf16[64,2304]{1,0:T(8,128)(2,1)S(1)}, u32[]{:S(2)}, u32[]{:S(2)}) collective-permute-start(bf16[64,2304]{1,0:T(8,128)(2,1)} %get-tuple-element.25), channel_id=1, source_target_pairs={{4,0},{6,2},{8,4},{10,6},{12,8},{14,10},{0,12},{2,14},{5,1},{7,3},... | collective-permute-start | bytes 884744 | tf_op jit(solution)/shard_map/ppermute | solution.py:221
  10.2 20.7 %collective-permute-start = (bf16[64,2304]{1,0:T(8,128)(2,1)}, bf16[64,2304]{1,0:T(8,128)(2,1)}, u32[]{:S(2)}, u32[]{:S(2)}) collective-permute-start(bf16[64,2304]{1,0:T(8,128)(2,1)} %get-tuple-element.25), channel_id=1, source_target_pairs={{2,0},{4,2},{6,4},{8,6},{10,8},{12,10},{14,12},{0,14},{3,1},{5,3},... | collective-permute-start | bytes 884744 | tf_op jit(solution)/shard_map/ppermute | solution.py:221
  12.0 20.5 %collective-permute-start.1 = (bf16[64,2304]{1,0:T(8,128)(2,1)}, bf16[64,2304]{1,0:T(8,128)(2,1)S(1)}, u32[]{:S(2)}, u32[]{:S(2)}) collective-permute-start(bf16[64,2304]{1,0:T(8,128)(2,1)} %get-tuple-element.25), channel_id=1, source_target_pairs={{14,0},{0,2},{2,4},{4,6},{6,8},{8,10},{10,12},{12,14},{15,1},{1,3}... | collective-permute-start | bytes 884744 | tf_op jit(solution)/shard_map/ppermute | solution.py:221
  12.0 26.5 %all-to-all-start = ((bf16[16,128,256]{2,1,0:T(8,128)(2,1)}), bf16[16,128,256]{2,1,0:T(8,128)(2,1)S(1)}, u32[]{:S(2)}, u32[]{:S(2)}) async-start(bf16[16,128,256]{2,1,0:T(8,128)(2,1)} %get-tuple-element.24), calls=%async_computation | async-start | bytes 2097152 | tf_op jit(solution)/shard_map/all_to_all | solution.py:235
  20.5 17.3 %collective-permute-start.5 = (bf16[64,2304]{1,0:T(8,128)(2,1)S(1)}, bf16[64,2304]{1,0:T(8,128)(2,1)S(1)}, u32[]{:S(2)}, u32[]{:S(2)}) collective-permute-start(bf16[64,2304]{1,0:T(8,128)(2,1)S(1)} %collective-permute-done.3), channel_id=1, source_target_pairs={{14,0},{0,2},{2,4},{4,6},{6,8},{8,10},{10,12},{12,14},{15,1},{1,3}... | collective-permute-start | bytes 884744 | tf_op jit(solution)/shard_map/ppermute | solution.py:221
  24.8 12.2 %collective-permute-start.4 = (bf16[64,2304]{1,0:T(8,128)(2,1)S(1)}, bf16[64,2304]{1,0:T(8,128)(2,1)S(1)}, u32[]{:S(2)}, u32[]{:S(2)}) collective-permute-start(bf16[64,2304]{1,0:T(8,128)(2,1)S(1)} %collective-permute-done.2), channel_id=1, source_target_pairs={{2,0},{4,2},{6,4},{8,6},{10,8},{12,10},{14,12},{0,14},{3,1},{5,3},... | collective-permute-start | bytes 884744 | tf_op jit(solution)/shard_map/ppermute | solution.py:221
  34.8 38.6 %copy-start = (s32[16]{0:T(128)S(1)}, s32[16]{0:T(128)}, u32[]{:S(2)}) copy-start(s32[16]{0:T(128)} %order_ref.3) | copy-start | bytes 196
  34.8 38.6 %copy-start.1 = (s32[16]{0:T(128)S(1)}, s32[16]{0:T(128)}, u32[]{:S(2)}) copy-start(s32[16]{0:T(128)} %length_ref.1) | copy-start | bytes 196
  38.6 33.6 %all-to-all-start.1 = ((bf16[16,64,512]{2,1,0:T(8,128)(2,1)}), bf16[16,64,512]{2,1,0:T(8,128)(2,1)S(1)}, u32[]{:S(2)}, u32[]{:S(2)}) async-start(bf16[16,64,512]{2,1,0:T(8,128)(2,1)} %bitcast.28), calls=%async_computation.1 | async-start | bytes 2097152 | tf_op jit(solution)/shard_map/all_to_all | solution.py:239
  46.2 43.9 %collective-permute-start.8 = (bf16[6,64,2304]{2,1,0:T(8,128)(2,1)}, bf16[6,64,2304]{2,1,0:T(8,128)(2,1)}, u32[]{:S(2)}, u32[]{:S(2)}) collective-permute-start(bf16[6,64,2304]{2,1,0:T(8,128)(2,1)} %bitcast_dynamic-update-slice_fusion.refs_0_), channel_id=1, source_target_pairs={{0,64},{64,128},{128,192},{192,0},{1,65},{65,129},{129,193},{193,1... | collective-permute-start | bytes 5308424 | tf_op jit(solution)/shard_map/ppermute | solution.py:228
  47.5 42.6 %collective-permute-start.7 = (bf16[6,64,2304]{2,1,0:T(8,128)(2,1)}, bf16[6,64,2304]{2,1,0:T(8,128)(2,1)}, u32[]{:S(2)}, u32[]{:S(2)}) collective-permute-start(bf16[6,64,2304]{2,1,0:T(8,128)(2,1)} %bitcast_dynamic-update-slice_fusion.refs_0_), channel_id=1, source_target_pairs={{0,192},{64,0},{128,64},{192,128},{1,193},{65,1},{129,65},{193,129... | collective-permute-start | bytes 5308424 | tf_op jit(solution)/shard_map/ppermute | solution.py:226
  48.9 61.0 %collective-permute-start.13 = (bf16[6,64,2304]{2,1,0:T(8,128)(2,1)}, bf16[6,64,2304]{2,1,0:T(8,128)(2,1)}, u32[]{:S(2)}, u32[]{:S(2)}) collective-permute-start(bf16[6,64,2304]{2,1,0:T(8,128)(2,1)} %bitcast_dynamic-update-slice_fusion.refs_0_), channel_id=1, source_target_pairs={{0,32},{32,0},{1,33},{33,1},{2,34},{34,2},{3,35},{35,3},{4,36},{36... | collective-permute-start | bytes 5308424 | tf_op jit(solution)/shard_map/ppermute | solution.py:227
  72.2 9.5 %collective-permute-start.6 = (bf16[64,2304]{1,0:T(8,128)(2,1)S(1)}, bf16[64,2304]{1,0:T(8,128)(2,1)S(1)}, u32[]{:S(2)}, u32[]{:S(2)}) collective-permute-start(bf16[64,2304]{1,0:T(8,128)(2,1)S(1)} %collective-permute-done.4), channel_id=1, source_target_pairs={{2,0},{4,2},{6,4},{8,6},{10,8},{12,10},{14,12},{0,14},{3,1},{5,3},... | collective-permute-start | bytes 884744 | tf_op jit(solution)/shard_map/ppermute | solution.py:221
  81.7 26.2 %all-to-all-start.2 = ((bf16[8,128,256]{2,1,0:T(8,128)(2,1)}), bf16[8,128,256]{2,1,0:T(8,128)(2,1)S(1)}, u32[]{:S(2)}, u32[]{:S(2)}) async-start(bf16[8,128,256]{2,1,0:T(8,128)(2,1)} %bitcast.16), calls=%async_computation.2 | async-start | bytes 1048576 | tf_op jit(solution)/shard_map/all_to_all | solution.py:250
  90.1 8.7 %collective-permute-start.11 = (bf16[1,64,2304]{2,1,0:T(8,128)(2,1)S(1)}, bf16[1,64,2304]{2,1,0:T(8,128)(2,1)S(1)}, u32[]{:S(2)}, u32[]{:S(2)}) collective-permute-start(bf16[1,64,2304]{2,1,0:T(8,128)(2,1)S(1)} %bitcast.31), channel_id=1, source_target_pairs={{0,64},{64,128},{128,192},{192,0},{1,65},{65,129},{129,193},{193,1... | collective-permute-start | bytes 884744 | tf_op jit(solution)/shard_map/ppermute | solution.py:228
  91.4 11.9 %collective-permute-start.10 = (bf16[1,64,2304]{2,1,0:T(8,128)(2,1)S(1)}, bf16[1,64,2304]{2,1,0:T(8,128)(2,1)S(1)}, u32[]{:S(2)}, u32[]{:S(2)}) collective-permute-start(bf16[1,64,2304]{2,1,0:T(8,128)(2,1)S(1)} %bitcast.32), channel_id=1, source_target_pairs={{0,32},{32,0},{1,33},{33,1},{2,34},{34,2},{3,35},{35,3},{4,36},{36... | collective-permute-start | bytes 884744 | tf_op jit(solution)/shard_map/ppermute | solution.py:227
  91.8 11.5 %collective-permute-start.9 = (bf16[1,64,2304]{2,1,0:T(8,128)(2,1)S(1)}, bf16[1,64,2304]{2,1,0:T(8,128)(2,1)S(1)}, u32[]{:S(2)}, u32[]{:S(2)}) collective-permute-start(bf16[1,64,2304]{2,1,0:T(8,128)(2,1)S(1)} %bitcast.33), channel_id=1, source_target_pairs={{0,192},{64,0},{128,64},{192,128},{1,193},{65,1},{129,65},{193,129... | collective-permute-start | bytes 884744 | tf_op jit(solution)/shard_map/ppermute | solution.py:226
  107.9 2.1 %collective-permute-start.12 = (bf16[8,128,256]{2,1,0:T(8,128)(2,1)S(1)}, bf16[8,128,256]{2,1,0:T(8,128)(2,1)S(1)}, u32[]{:S(2)}, u32[]{:S(2)}) collective-permute-start(bf16[8,128,256]{2,1,0:T(8,128)(2,1)S(1)} %all-to-all-done.2.own_ref), channel_id=1, source_target_pairs={{0,16},{16,0},{1,17},{17,1},{2,18},{18,2},{3,19},{19,3},{4,20},{20... | collective-permute-start | bytes 1572872 | tf_op jit(solution)/shard_map/ppermute | solution.py:254
  115.7 16.1 %collective-permute-start.14 = (bf16[128,2304]{1,0:T(8,128)(2,1)S(1)}, bf16[128,2304]{1,0:T(8,128)(2,1)S(1)}, u32[]{:S(2)}, u32[]{:S(2)}) collective-permute-start(bf16[128,2304]{1,0:T(8,128)(2,1)S(1)} %get-tuple-element.41), channel_id=1, source_target_pairs={{0,1},{1,0},{2,3},{3,2},{4,5},{5,4},{6,7},{7,6},{8,9},{9,8},{10,11... | collective-permute-start | bytes 1769480 | tf_op jit(solution)/shard_map/ppermute | solution.py:258
  132.0 2.8 %copy-start.3 = (bf16[1,64,4608]{2,1,0:T(8,128)(2,1)S(1)}, bf16[1,64,4608]{2,1,0:T(8,128)(2,1)}, u32[]{:S(2)}) copy-start(bf16[1,64,4608]{2,1,0:T(8,128)(2,1)} %param.7) | copy-start | bytes 1769476
  132.0 2.8 %copy-start.4 = (f32[4608]{0:T(1024)S(1)}, f32[4608]{0:T(1024)}, u32[]{:S(2)}) copy-start(f32[4608]{0:T(1024)} %param.13) | copy-start | bytes 55300
  132.0 2.5 %collective-permute-start.15 = (bf16[64,2304]{1,0:T(8,128)(2,1)S(1)}, bf16[64,2304]{1,0:T(8,128)(2,1)S(1)}, u32[]{:S(2)}, u32[]{:S(2)}) collective-permute-start(bf16[64,2304]{1,0:T(8,128)(2,1)S(1)} %slice.14), channel_id=1, source_target_pairs={{0,16},{16,0},{1,17},{17,1},{2,18},{18,2},{3,19},{19,3},{4,20},{20... | collective-permute-start | bytes 884744 | tf_op jit(solution)/shard_map/ppermute | solution.py:260

commit v5 on v4

--- a/solution.py
+++ b/solution.py
@@ -136,7 +136,7 @@
 
 
 def project_kernel(spot_ref, own_ref, other_ref, local, *refs):
-    weights, (send_ref, keep_ref, total) = refs[:-3], refs[-3:]
+    weights, (send_ref, send_other_ref, keep_ref, total) = refs[:-4], refs[-4:]
     blocks = own_ref.shape[0]
     rows, cols = local.shape
     quarter = rows // 4
@@ -169,7 +169,8 @@
             if r < blocks - 1:
                 total[:, at] = part
             else:
-                send_ref[:, at] = part[: 2 * half].astype(jnp.bfloat16)
+                send_ref[:, at] = part[:half].astype(jnp.bfloat16)
+                send_other_ref[:, at] = part[half : 2 * half].astype(jnp.bfloat16)
                 keep_ref[:, at] = part[2 * half :]
 
 
@@ -180,11 +181,12 @@
     return pl.pallas_call(
         project_kernel,
         out_shape=(
-            jax.ShapeDtypeStruct((tokens, cols), jnp.bfloat16),
+            jax.ShapeDtypeStruct((tokens // 2, cols), jnp.bfloat16),
+            jax.ShapeDtypeStruct((tokens // 2, cols), jnp.bfloat16),
             jax.ShapeDtypeStruct((tokens, cols), jnp.float32),
         ),
         in_specs=[pl.BlockSpec(memory_space=pltpu.SMEM)] + [vmem] * (3 + len(weights)),
-        out_specs=(vmem, vmem),
+        out_specs=(vmem, vmem, vmem),
         scratch_shapes=[
             pltpu.VMEM((2 * tokens, cols), jnp.float32),
         ],
@@ -254,10 +256,11 @@
     other = lax.ppermute(own, "core", swap)
     spots = jnp.stack([yh, lax.axis_index("z"), color]).astype(jnp.int32)
     local = lax.dynamic_slice(out_weight, (0, core * half_cols), (rows_here, half_cols))
-    send, keep = project(spots, own, other, local, weights + last)
-    summed = lax.ppermute(send, "yh", swap).astype(jnp.float32) + keep
-    mine, theirs = summed[:per_device], summed[per_device:]
+    send, send_other, keep = project(spots, own, other, local, weights + last)
+    theirs = lax.ppermute(send_other, "yh", swap)
+    theirs = theirs.astype(jnp.float32) + keep[per_device:]
     back = lax.ppermute(theirs.astype(jnp.bfloat16), "core", swap).astype(jnp.float32)
+    mine = lax.ppermute(send, "yh", swap).astype(jnp.float32) + keep[:per_device]
     first = core == 0
     projected = jnp.concatenate(
         [jnp.where(first, mine, back), jnp.where(first, back, mine)], axis=1

time: 136 us -> 134 us (0.985)
  waiting for transfers between devices: 63 us -> 57.3 us
  starting transfers between devices: 45.6 us -> 48.7 us
    ppermute x1 -> x2, waiting for transfers between devices: 15.4 us -> 10.9 us  [the longest x1 6.76 us: body(): theirs = lax.ppermute(send_other, 'yh', swap)]
    ppermute x1 -> x2, starting transfers between devices: 0.72 us -> 2.97 us  [the longest x1 2.34 us: body(): lax.ppermute(send, 'yh', swap).astype(jnp.float32) + keep[:per_device]]
  transfers between devices with their start and end apart: 19 -> 20, of which waited for: 10 -> 10; matrix products, arithmetic and copies ran while one was open for 6% -> 6% of each run, Pallas kernels for 6% -> 6%
where the time goes in v5:
time: 134 us
  waiting for transfers between devices  57.3 us (43%)
  starting transfers between devices  48.7 us (36%)
  Pallas kernels  17.8 us (13%)
  local copies, waits for them, and re-layouts  8.35 us (6%)
  other arithmetic  1.57 us (1%)
    all_to_all x1, waiting for transfers between devices, body(): qkv = lax.all_to_all(by_head, SEQ, 0, 0, tiled=True).reshape(-1, width)  22.8 us
    ppermute x7, starting transfers between devices, from_z(): lax.ppermute(block, 'z', [((i + distance) % nz, i) for i in range(nz)])  13.9 us
    ppermute x7, waiting for transfers between devices, from_z(): lax.ppermute(block, 'z', [((i + distance) % nz, i) for i in range(nz)])  8.72 us
    all_to_all x1, starting transfers between devices, body(): lax.all_to_all(attended.reshape(nz, -1, attended.shape[-1]), 'z', 0, 0, t...  8.37 us
    pallas_call x1, Pallas kernels, attend(): pl.pallas_call(functools.partial(attend_kernel, block=block, chunk=chunk)...  8.32 us
    all_to_all x1, starting transfers between devices, body(): qkv = lax.all_to_all(by_head, SEQ, 0, 0, tiled=True).reshape(-1, width)  7.62 us
    all_to_all x1, starting transfers between devices, body(): prompts = lax.all_to_all(picked, GROUP, 0, 0, tiled=True)  6.84 us
    ppermute x1, waiting for transfers between devices, body(): theirs = lax.ppermute(send_other, 'yh', swap)  6.76 us
  transfers between devices with their start and end apart: 20, of which 10 were waited for; matrix products, arithmetic and copies ran while one was open for 6% of the time, Pallas kernels for 6%

profile of v5, /device:TPU:1, one launch (start us, length us, event | category | flops | bytes accessed | tf_op | source)
XLA Modules:
  0.0 133.8 jit_solution(16220255079130242493)
XLA Ops:
  0.0 3.2 %prepare.1 = (bf16[16,128,256]{2,1,0:T(8,128)(2,1)}, bf16[64,2304]{1,0:T(8,128)(2,1)}) custom-call(s32[16]{0:T(128)} %order_ref.3, bf16[16,128,256]{2,1,0:T(8,128)(2,1)} %bitcast.37, bf16[256,4608]{1,0:T(8,128)(2,1)} %weight_ref.1), custom_call_target="tpu_custom_call" | custom-call | tf_op jit(solution)/shard_map/prepare/pallas_call | solution.py:46
  3.2 0.0 copy-start.2
  3.2 3.9 %collective-permute-start.3 = (bf16[64,2304]{1,0:T(8,128)(2,1)}, bf16[64,2304]{1,0:T(8,128)(2,1)S(1)}, u32[]{:S(2)}, u32[]{:S(2)}) collective-permute-start(bf16[64,2304]{1,0:T(8,128)(2,1)} %get-tuple-element.26), channel_id=1, source_target_pairs={{12,0},{14,2},{0,4},{2,6},{4,8},{6,10},{8,12},{10,14},{13,1},{15,3... | collective-permute-start | bytes 884744 | tf_op jit(solution)/shard_map/ppermute | solution.py:223
  7.1 3.1 %collective-permute-start.2 = (bf16[64,2304]{1,0:T(8,128)(2,1)}, bf16[64,2304]{1,0:T(8,128)(2,1)S(1)}, u32[]{:S(2)}, u32[]{:S(2)}) collective-permute-start(bf16[64,2304]{1,0:T(8,128)(2,1)} %get-tuple-element.26), channel_id=1, source_target_pairs={{4,0},{6,2},{8,4},{10,6},{12,8},{14,10},{0,12},{2,14},{5,1},{7,3},... | collective-permute-start | bytes 884744 | tf_op jit(solution)/shard_map/ppermute | solution.py:223
  10.2 1.8 %collective-permute-start = (bf16[64,2304]{1,0:T(8,128)(2,1)}, bf16[64,2304]{1,0:T(8,128)(2,1)}, u32[]{:S(2)}, u32[]{:S(2)}) collective-permute-start(bf16[64,2304]{1,0:T(8,128)(2,1)} %get-tuple-element.26), channel_id=1, source_target_pairs={{2,0},{4,2},{6,4},{8,6},{10,8},{12,10},{14,12},{0,14},{3,1},{5,3},... | collective-permute-start | bytes 884744 | tf_op jit(solution)/shard_map/ppermute | solution.py:223
  12.0 0.0 collective-permute-start.1
  12.0 6.8 %all-to-all-start = ((bf16[16,128,256]{2,1,0:T(8,128)(2,1)}), bf16[16,128,256]{2,1,0:T(8,128)(2,1)S(1)}, u32[]{:S(2)}, u32[]{:S(2)}) async-start(bf16[16,128,256]{2,1,0:T(8,128)(2,1)} %get-tuple-element.25), calls=%async_computation | async-start | bytes 2097152 | tf_op jit(solution)/shard_map/all_to_all | solution.py:237
  18.9 0.0 copy-done.2
  18.9 1.6 %copy.11 = bf16[1,64,16,512]{3,1,2,0:T(8,128)(2,1)} copy(bf16[1,64,16,512]{3,2,1,0:T(8,128)(2,1)S(1)} %copy-done.2) | data formatting | bytes 2097152 | tf_op args[1]
  20.5 0.0 collective-permute-done.3
  20.5 3.9 %collective-permute-start.5 = (bf16[64,2304]{1,0:T(8,128)(2,1)S(1)}, bf16[64,2304]{1,0:T(8,128)(2,1)S(1)}, u32[]{:S(2)}, u32[]{:S(2)}) collective-permute-start(bf16[64,2304]{1,0:T(8,128)(2,1)S(1)} %collective-permute-done.3), channel_id=1, source_target_pairs={{14,0},{0,2},{2,4},{4,6},{6,8},{8,10},{10,12},{12,14},{15,1},{1,3}... | collective-permute-start | bytes 884744 | tf_op jit(solution)/shard_map/ppermute | solution.py:223
  24.4 0.4 collective-permute-done.2
  24.8 0.0 collective-permute-start.4
  24.8 6.0 %collective-permute-done = bf16[64,2304]{1,0:T(8,128)(2,1)} collective-permute-done((bf16[64,2304]{1,0:T(8,128)(2,1)}, bf16[64,2304]{1,0:T(8,128)(2,1)}, u32[]{:S(2)}, u32[]{:S(2)}) %collective-permute-start) | collective-permute-done | bytes 294944 | tf_op jit(solution)/shard_map/ppermute | solution.py:223
  30.9 1.7 %bitcast_dynamic-update-slice_fusion.5 = bf16[6,64,2304]{2,1,0:T(8,128)(2,1)} fusion(bf16[64,2304]{1,0:T(8,128)(2,1)} %collective-permute-done), kind=kLoop, calls=%fused_computation.16 | loop fusion | bytes 589824
  32.6 0.0 collective-permute-done.1
  32.6 0.7 bitcast_dynamic-update-slice_fusion.4
  33.3 0.7 bitcast_dynamic-update-slice_fusion.3
  34.0 0.7 bitcast_dynamic-update-slice_fusion.2
  34.8 0.0 copy-start
  34.8 2.3 %collective-permute-done.4 = bf16[64,2304]{1,0:T(8,128)(2,1)S(1)} collective-permute-done((bf16[64,2304]{1,0:T(8,128)(2,1)S(1)}, bf16[64,2304]{1,0:T(8,128)(2,1)S(1)}, u32[]{:S(2)}, u32[]{:S(2)}) %collective-permute-start.4) | collective-permute-done | bytes 294944 | tf_op jit(solution)/shard_map/ppermute | solution.py:223
  37.1 0.7 bitcast_dynamic-update-slice_fusion.1
  37.8 0.0 collective-permute-done.5
  37.8 0.7 bitcast_dynamic-update-slice_fusion.refs_0_
  38.5 0.0 all-to-all-done
  38.5 7.6 %all-to-all-start.1 = ((bf16[16,64,512]{2,1,0:T(8,128)(2,1)}), bf16[16,64,512]{2,1,0:T(8,128)(2,1)S(1)}, u32[]{:S(2)}, u32[]{:S(2)}) async-start(bf16[16,64,512]{2,1,0:T(8,128)(2,1)} %bitcast.28), calls=%async_computation.1 | async-start | bytes 2097152 | tf_op jit(solution)/shard_map/all_to_all | solution.py:241
  46.2 1.3 collective-permute-start.8
  47.5 1.5 %collective-permute-start.7 = (bf16[6,64,2304]{2,1,0:T(8,128)(2,1)}, bf16[6,64,2304]{2,1,0:T(8,128)(2,1)}, u32[]{:S(2)}, u32[]{:S(2)}) collective-permute-start(bf16[6,64,2304]{2,1,0:T(8,128)(2,1)} %bitcast_dynamic-update-slice_fusion.refs_0_), channel_id=1, source_target_pairs={{0,192},{64,0},{128,64},{192,128},{1,193},{65,1},{129,65},{193,129... | collective-permute-start | bytes 5308424 | tf_op jit(solution)/shard_map/ppermute | solution.py:228
  48.9 0.4 collective-permute-start.13
  49.3 22.8 %all-to-all-done.1 = bf16[16,64,512]{2,1,0:T(8,128)(2,1)S(1)} async-done(((bf16[16,64,512]{2,1,0:T(8,128)(2,1)}), bf16[16,64,512]{2,1,0:T(8,128)(2,1)S(1)}, u32[]{:S(2)}, u32[]{:S(2)}) %all-to-all-start.1) | async-done | bytes 1048608 | tf_op jit(solution)/shard_map/all_to_all | solution.py:241
  72.1 1.1 collective-permute-start.6
  73.3 0.1 pad_add_fusion.1.spot_ref
  73.3 0.0 copy-done
  73.3 0.0 copy-done.1
  73.3 8.3 %attend.1 = bf16[1024,256]{1,0:T(8,128)(2,1)} custom-call(s32[2]{0:T(128)S(1)} %pad_add_fusion.1.spot_ref, s32[16]{0:T(128)S(1)} %copy-done, s32[16]{0:T(128)S(1)} %copy-done.1, bf16[1024,512]{1,0:T(8,128)(2,1)S(1)} %bitcast.30, bf16[2048,256]{1,0:T(8,128)(2,1)S(1)} %bitcast.29), custom_call_target="tpu_custom_call" | custom-call | flops 1000000 | bytes 65536 | tf_op jit(solution)/shard_map/attend/pallas_call | solution.py:121
  81.7 0.0 collective-permute-done.6
  81.7 8.4 %all-to-all-start.2 = ((bf16[8,128,256]{2,1,0:T(8,128)(2,1)}), bf16[8,128,256]{2,1,0:T(8,128)(2,1)S(1)}, u32[]{:S(2)}, u32[]{:S(2)}) async-start(bf16[8,128,256]{2,1,0:T(8,128)(2,1)} %bitcast.16), calls=%async_computation.2 | async-start | bytes 1048576 | tf_op jit(solution)/shard_map/all_to_all | solution.py:252
  90.0 0.0 collective-permute-done.8.refs_3_
  90.0 0.0 collective-permute-done.7.refs_1_
  90.0 1.3 collective-permute-start.11
  91.3 0.4 collective-permute-start.10
  91.7 1.5 %collective-permute-start.9 = (bf16[1,64,2304]{2,1,0:T(8,128)(2,1)S(1)}, bf16[1,64,2304]{2,1,0:T(8,128)(2,1)S(1)}, u32[]{:S(2)}, u32[]{:S(2)}) collective-permute-start(bf16[1,64,2304]{2,1,0:T(8,128)(2,1)S(1)} %bitcast.33), channel_id=1, source_target_pairs={{0,192},{64,0},{128,64},{192,128},{1,193},{65,1},{129,65},{193,129... | collective-permute-start | bytes 884744 | tf_op jit(solution)/shard_map/ppermute | solution.py:228
  93.2 5.5 %collective-permute-done.11.refs_7_ = bf16[1,64,2304]{2,1,0:T(8,128)(2,1)S(1)} collective-permute-done((bf16[1,64,2304]{2,1,0:T(8,128)(2,1)S(1)}, bf16[1,64,2304]{2,1,0:T(8,128)(2,1)S(1)}, u32[]{:S(2)}, u32[]{:S(2)}) %collective-permute-start.11) | collective-permute-done | bytes 294944 | tf_op jit(solution)/shard_map/ppermute | solution.py:230
  98.7 4.5 %collective-permute-done.10.refs_6_ = bf16[1,64,2304]{2,1,0:T(8,128)(2,1)S(1)} collective-permute-done((bf16[1,64,2304]{2,1,0:T(8,128)(2,1)S(1)}, bf16[1,64,2304]{2,1,0:T(8,128)(2,1)S(1)}, u32[]{:S(2)}, u32[]{:S(2)}) %collective-permute-start.10) | collective-permute-done | bytes 294944 | tf_op jit(solution)/shard_map/ppermute | solution.py:229
  103.3 0.0 collective-permute-done.9.refs_5_
  103.3 4.6 %all-to-all-done.2.own_ref = bf16[8,128,256]{2,1,0:T(8,128)(2,1)S(1)} async-done(((bf16[8,128,256]{2,1,0:T(8,128)(2,1)}), bf16[8,128,256]{2,1,0:T(8,128)(2,1)S(1)}, u32[]{:S(2)}, u32[]{:S(2)}) %all-to-all-start.2) | async-done | bytes 524320 | tf_op jit(solution)/shard_map/all_to_all | solution.py:252
  107.9 0.6 collective-permute-start.12
  108.5 0.1 pad_add_fusion.spot_ref
  108.6 1.3 %constant_dynamic-slice_fusion.local = bf16[256,2304]{1,0:T(8,128)(2,1)S(1)} fusion(bf16[256,4608]{1,0:T(8,128)(2,1)} %weight_ref.1, s32[]{:T(128)S(6)} %select_n.29), kind=kLoop, calls=%fused_computation.20 | loop fusion | bytes 2359300 | tf_op jit(solution)/shard_map/dynamic_slice | solution.py:258
  109.9 0.0 collective-permute-done.13.refs_2_
  109.9 0.1 collective-permute-done.12.other_ref
  110.0 6.4 %project.1 = (bf16[64,2304]{1,0:T(8,128)(2,1)}, bf16[64,2304]{1,0:T(8,128)(2,1)S(1)}, f32[128,2304]{1,0:T(8,128)S(1)}) custom-call(s32[3]{0:T(128)S(1)} %pad_add_fusion.spot_ref, bf16[8,128,256]{2,1,0:T(8,128)(2,1)S(1)} %all-to-all-done.2.own_ref, bf16[8,128,256]{2,1,0:T(8,128)(2,1)S(1)} %collective-permute-done.12.other_ref, ...), custom_call_target="tpu_custom_call" | custom-call | flops 2415919104 | bytes 12582912 | tf_op jit(solution)/shard_map/project/pallas_call | solution.py:181
  116.4 0.6 collective-permute-start.15
  117.0 2.3 %collective-permute-start.14 = (bf16[64,2304]{1,0:T(8,128)(2,1)}, bf16[64,2304]{1,0:T(8,128)(2,1)S(1)}, u32[]{:S(2)}, u32[]{:S(2)}) collective-permute-start(bf16[64,2304]{1,0:T(8,128)(2,1)} %get-tuple-element.42), channel_id=1, source_target_pairs={{0,1},{1,0},{2,3},{3,2},{4,5},{5,4},{6,7},{7,6},{8,9},{9,8},{10,11... | collective-permute-start | bytes 884744 | tf_op jit(solution)/shard_map/ppermute | solution.py:263
  119.4 6.8 %collective-permute-done.15 = bf16[64,2304]{1,0:T(8,128)(2,1)S(1)} collective-permute-done((bf16[64,2304]{1,0:T(8,128)(2,1)S(1)}, bf16[64,2304]{1,0:T(8,128)(2,1)S(1)}, u32[]{:S(2)}, u32[]{:S(2)}) %collective-permute-start.15) | collective-permute-done | bytes 294944 | tf_op jit(solution)/shard_map/ppermute | solution.py:260
  126.1 0.1 add_convert_fusion
  126.2 2.1 %collective-permute-start.16 = (bf16[64,2304]{1,0:T(8,128)(2,1)S(1)}, bf16[64,2304]{1,0:T(8,128)(2,1)S(1)}, u32[]{:S(2)}, u32[]{:S(2)}) collective-permute-start(bf16[64,2304]{1,0:T(8,128)(2,1)S(1)} %add_convert_fusion), channel_id=1, source_target_pairs={{0,16},{16,0},{1,17},{17,1},{2,18},{18,2},{3,19},{19,3},{4,20},{20... | collective-permute-start | bytes 884744 | tf_op jit(solution)/shard_map/ppermute | solution.py:262
  128.3 4.2 %collective-permute-done.14 = bf16[64,2304]{1,0:T(8,128)(2,1)S(1)} collective-permute-done((bf16[64,2304]{1,0:T(8,128)(2,1)}, bf16[64,2304]{1,0:T(8,128)(2,1)S(1)}, u32[]{:S(2)}, u32[]{:S(2)}) %collective-permute-start.14) | collective-permute-done | bytes 294944 | tf_op jit(solution)/shard_map/ppermute | solution.py:263
  132.4 0.0 collective-permute-done.16
  132.4 0.1 convert_select_fusion.1
  132.5 0.2 fusion.3
  132.7 0.0 copy-done.3
  132.8 0.0 copy-done.4
  132.8 1.1 fusion.2
  (4 shorter events, 0.0 us)
Async XLA Ops:
  3.2 15.7 %copy-start.2 = (bf16[1,64,16,512]{3,2,1,0:T(8,128)(2,1)S(1)}, bf16[1,64,16,512]{3,2,1,0:T(8,128)(2,1)}, u32[]{:S(2)}) copy-start(bf16[1,64,16,512]{3,2,1,0:T(8,128)(2,1)} %param.8) | copy-start | bytes 3145732
  3.2 17.3 %collective-permute-start.3 = (bf16[64,2304]{1,0:T(8,128)(2,1)}, bf16[64,2304]{1,0:T(8,128)(2,1)S(1)}, u32[]{:S(2)}, u32[]{:S(2)}) collective-permute-start(bf16[64,2304]{1,0:T(8,128)(2,1)} %get-tuple-element.26), channel_id=1, source_target_pairs={{12,0},{14,2},{0,4},{2,6},{4,8},{6,10},{8,12},{10,14},{13,1},{15,3... | collective-permute-start | bytes 884744 | tf_op jit(solution)/shard_map/ppermute | solution.py:223
  7.1 17.8 %collective-permute-start.2 = (bf16[64,2304]{1,0:T(8,128)(2,1)}, bf16[64,2304]{1,0:T(8,128)(2,1)S(1)}, u32[]{:S(2)}, u32[]{:S(2)}) collective-permute-start(bf16[64,2304]{1,0:T(8,128)(2,1)} %get-tuple-element.26), channel_id=1, source_target_pairs={{4,0},{6,2},{8,4},{10,6},{12,8},{14,10},{0,12},{2,14},{5,1},{7,3},... | collective-permute-start | bytes 884744 | tf_op jit(solution)/shard_map/ppermute | solution.py:223
  10.2 20.7 %collective-permute-start = (bf16[64,2304]{1,0:T(8,128)(2,1)}, bf16[64,2304]{1,0:T(8,128)(2,1)}, u32[]{:S(2)}, u32[]{:S(2)}) collective-permute-start(bf16[64,2304]{1,0:T(8,128)(2,1)} %get-tuple-element.26), channel_id=1, source_target_pairs={{2,0},{4,2},{6,4},{8,6},{10,8},{12,10},{14,12},{0,14},{3,1},{5,3},... | collective-permute-start | bytes 884744 | tf_op jit(solution)/shard_map/ppermute | solution.py:223
  12.0 20.5 %collective-permute-start.1 = (bf16[64,2304]{1,0:T(8,128)(2,1)}, bf16[64,2304]{1,0:T(8,128)(2,1)S(1)}, u32[]{:S(2)}, u32[]{:S(2)}) collective-permute-start(bf16[64,2304]{1,0:T(8,128)(2,1)} %get-tuple-element.26), channel_id=1, source_target_pairs={{14,0},{0,2},{2,4},{4,6},{6,8},{8,10},{10,12},{12,14},{15,1},{1,3}... | collective-permute-start | bytes 884744 | tf_op jit(solution)/shard_map/ppermute | solution.py:223
  12.0 26.5 %all-to-all-start = ((bf16[16,128,256]{2,1,0:T(8,128)(2,1)}), bf16[16,128,256]{2,1,0:T(8,128)(2,1)S(1)}, u32[]{:S(2)}, u32[]{:S(2)}) async-start(bf16[16,128,256]{2,1,0:T(8,128)(2,1)} %get-tuple-element.25), calls=%async_computation | async-start | bytes 2097152 | tf_op jit(solution)/shard_map/all_to_all | solution.py:237
  20.5 17.3 %collective-permute-start.5 = (bf16[64,2304]{1,0:T(8,128)(2,1)S(1)}, bf16[64,2304]{1,0:T(8,128)(2,1)S(1)}, u32[]{:S(2)}, u32[]{:S(2)}) collective-permute-start(bf16[64,2304]{1,0:T(8,128)(2,1)S(1)} %collective-permute-done.3), channel_id=1, source_target_pairs={{14,0},{0,2},{2,4},{4,6},{6,8},{8,10},{10,12},{12,14},{15,1},{1,3}... | collective-permute-start | bytes 884744 | tf_op jit(solution)/shard_map/ppermute | solution.py:223
  24.8 12.2 %collective-permute-start.4 = (bf16[64,2304]{1,0:T(8,128)(2,1)S(1)}, bf16[64,2304]{1,0:T(8,128)(2,1)S(1)}, u32[]{:S(2)}, u32[]{:S(2)}) collective-permute-start(bf16[64,2304]{1,0:T(8,128)(2,1)S(1)} %collective-permute-done.2), channel_id=1, source_target_pairs={{2,0},{4,2},{6,4},{8,6},{10,8},{12,10},{14,12},{0,14},{3,1},{5,3},... | collective-permute-start | bytes 884744 | tf_op jit(solution)/shard_map/ppermute | solution.py:223
  34.8 38.6 %copy-start = (s32[16]{0:T(128)S(1)}, s32[16]{0:T(128)}, u32[]{:S(2)}) copy-start(s32[16]{0:T(128)} %order_ref.3) | copy-start | bytes 196
  34.8 38.6 %copy-start.1 = (s32[16]{0:T(128)S(1)}, s32[16]{0:T(128)}, u32[]{:S(2)}) copy-start(s32[16]{0:T(128)} %length_ref.1) | copy-start | bytes 196
  38.5 33.6 %all-to-all-start.1 = ((bf16[16,64,512]{2,1,0:T(8,128)(2,1)}), bf16[16,64,512]{2,1,0:T(8,128)(2,1)S(1)}, u32[]{:S(2)}, u32[]{:S(2)}) async-start(bf16[16,64,512]{2,1,0:T(8,128)(2,1)} %bitcast.28), calls=%async_computation.1 | async-start | bytes 2097152 | tf_op jit(solution)/shard_map/all_to_all | solution.py:241
  46.2 43.9 %collective-permute-start.8 = (bf16[6,64,2304]{2,1,0:T(8,128)(2,1)}, bf16[6,64,2304]{2,1,0:T(8,128)(2,1)}, u32[]{:S(2)}, u32[]{:S(2)}) collective-permute-start(bf16[6,64,2304]{2,1,0:T(8,128)(2,1)} %bitcast_dynamic-update-slice_fusion.refs_0_), channel_id=1, source_target_pairs={{0,64},{64,128},{128,192},{192,0},{1,65},{65,129},{129,193},{193,1... | collective-permute-start | bytes 5308424 | tf_op jit(solution)/shard_map/ppermute | solution.py:230
  47.5 42.6 %collective-permute-start.7 = (bf16[6,64,2304]{2,1,0:T(8,128)(2,1)}, bf16[6,64,2304]{2,1,0:T(8,128)(2,1)}, u32[]{:S(2)}, u32[]{:S(2)}) collective-permute-start(bf16[6,64,2304]{2,1,0:T(8,128)(2,1)} %bitcast_dynamic-update-slice_fusion.refs_0_), channel_id=1, source_target_pairs={{0,192},{64,0},{128,64},{192,128},{1,193},{65,1},{129,65},{193,129... | collective-permute-start | bytes 5308424 | tf_op jit(solution)/shard_map/ppermute | solution.py:228
  48.9 61.0 %collective-permute-start.13 = (bf16[6,64,2304]{2,1,0:T(8,128)(2,1)}, bf16[6,64,2304]{2,1,0:T(8,128)(2,1)}, u32[]{:S(2)}, u32[]{:S(2)}) collective-permute-start(bf16[6,64,2304]{2,1,0:T(8,128)(2,1)} %bitcast_dynamic-update-slice_fusion.refs_0_), channel_id=1, source_target_pairs={{0,32},{32,0},{1,33},{33,1},{2,34},{34,2},{3,35},{35,3},{4,36},{36... | collective-permute-start | bytes 5308424 | tf_op jit(solution)/shard_map/ppermute | solution.py:229
  72.1 9.5 %collective-permute-start.6 = (bf16[64,2304]{1,0:T(8,128)(2,1)S(1)}, bf16[64,2304]{1,0:T(8,128)(2,1)S(1)}, u32[]{:S(2)}, u32[]{:S(2)}) collective-permute-start(bf16[64,2304]{1,0:T(8,128)(2,1)S(1)} %collective-permute-done.4), channel_id=1, source_target_pairs={{2,0},{4,2},{6,4},{8,6},{10,8},{12,10},{14,12},{0,14},{3,1},{5,3},... | collective-permute-start | bytes 884744 | tf_op jit(solution)/shard_map/ppermute | solution.py:223
  81.7 26.2 %all-to-all-start.2 = ((bf16[8,128,256]{2,1,0:T(8,128)(2,1)}), bf16[8,128,256]{2,1,0:T(8,128)(2,1)S(1)}, u32[]{:S(2)}, u32[]{:S(2)}) async-start(bf16[8,128,256]{2,1,0:T(8,128)(2,1)} %bitcast.16), calls=%async_computation.2 | async-start | bytes 1048576 | tf_op jit(solution)/shard_map/all_to_all | solution.py:252
  90.0 8.7 %collective-permute-start.11 = (bf16[1,64,2304]{2,1,0:T(8,128)(2,1)S(1)}, bf16[1,64,2304]{2,1,0:T(8,128)(2,1)S(1)}, u32[]{:S(2)}, u32[]{:S(2)}) collective-permute-start(bf16[1,64,2304]{2,1,0:T(8,128)(2,1)S(1)} %bitcast.31), channel_id=1, source_target_pairs={{0,64},{64,128},{128,192},{192,0},{1,65},{65,129},{129,193},{193,1... | collective-permute-start | bytes 884744 | tf_op jit(solution)/shard_map/ppermute | solution.py:230
  91.3 11.9 %collective-permute-start.10 = (bf16[1,64,2304]{2,1,0:T(8,128)(2,1)S(1)}, bf16[1,64,2304]{2,1,0:T(8,128)(2,1)S(1)}, u32[]{:S(2)}, u32[]{:S(2)}) collective-permute-start(bf16[1,64,2304]{2,1,0:T(8,128)(2,1)S(1)} %bitcast.32), channel_id=1, source_target_pairs={{0,32},{32,0},{1,33},{33,1},{2,34},{34,2},{3,35},{35,3},{4,36},{36... | collective-permute-start | bytes 884744 | tf_op jit(solution)/shard_map/ppermute | solution.py:229
  91.7 11.5 %collective-permute-start.9 = (bf16[1,64,2304]{2,1,0:T(8,128)(2,1)S(1)}, bf16[1,64,2304]{2,1,0:T(8,128)(2,1)S(1)}, u32[]{:S(2)}, u32[]{:S(2)}) collective-permute-start(bf16[1,64,2304]{2,1,0:T(8,128)(2,1)S(1)} %bitcast.33), channel_id=1, source_target_pairs={{0,192},{64,0},{128,64},{192,128},{1,193},{65,1},{129,65},{193,129... | collective-permute-start | bytes 884744 | tf_op jit(solution)/shard_map/ppermute | solution.py:228
  107.9 2.1 %collective-permute-start.12 = (bf16[8,128,256]{2,1,0:T(8,128)(2,1)S(1)}, bf16[8,128,256]{2,1,0:T(8,128)(2,1)S(1)}, u32[]{:S(2)}, u32[]{:S(2)}) collective-permute-start(bf16[8,128,256]{2,1,0:T(8,128)(2,1)S(1)} %all-to-all-done.2.own_ref), channel_id=1, source_target_pairs={{0,16},{16,0},{1,17},{17,1},{2,18},{18,2},{3,19},{19,3},{4,20},{20... | collective-permute-start | bytes 1572872 | tf_op jit(solution)/shard_map/ppermute | solution.py:256
  116.4 9.7 %collective-permute-start.15 = (bf16[64,2304]{1,0:T(8,128)(2,1)S(1)}, bf16[64,2304]{1,0:T(8,128)(2,1)S(1)}, u32[]{:S(2)}, u32[]{:S(2)}) collective-permute-start(bf16[64,2304]{1,0:T(8,128)(2,1)S(1)} %get-tuple-element.44), channel_id=1, source_target_pairs={{0,1},{1,0},{2,3},{3,2},{4,5},{5,4},{6,7},{7,6},{8,9},{9,8},{10,11... | collective-permute-start | bytes 884744 | tf_op jit(solution)/shard_map/ppermute | solution.py:260
  117.0 15.4 %collective-permute-start.14 = (bf16[64,2304]{1,0:T(8,128)(2,1)}, bf16[64,2304]{1,0:T(8,128)(2,1)S(1)}, u32[]{:S(2)}, u32[]{:S(2)}) collective-permute-start(bf16[64,2304]{1,0:T(8,128)(2,1)} %get-tuple-element.42), channel_id=1, source_target_pairs={{0,1},{1,0},{2,3},{3,2},{4,5},{5,4},{6,7},{7,6},{8,9},{9,8},{10,11... | collective-permute-start | bytes 884744 | tf_op jit(solution)/shard_map/ppermute | solution.py:263
  126.2 6.3 %collective-permute-start.16 = (bf16[64,2304]{1,0:T(8,128)(2,1)S(1)}, bf16[64,2304]{1,0:T(8,128)(2,1)S(1)}, u32[]{:S(2)}, u32[]{:S(2)}) collective-permute-start(bf16[64,2304]{1,0:T(8,128)(2,1)S(1)} %add_convert_fusion), channel_id=1, source_target_pairs={{0,16},{16,0},{1,17},{17,1},{2,18},{18,2},{3,19},{19,3},{4,20},{20... | collective-permute-start | bytes 884744 | tf_op jit(solution)/shard_map/ppermute | solution.py:262
  128.3 4.5 %copy-start.3 = (bf16[1,64,4608]{2,1,0:T(8,128)(2,1)S(1)}, bf16[1,64,4608]{2,1,0:T(8,128)(2,1)}, u32[]{:S(2)}) copy-start(bf16[1,64,4608]{2,1,0:T(8,128)(2,1)} %param.7) | copy-start | bytes 1769476
  128.3 4.5 %copy-start.4 = (f32[4608]{0:T(1024)S(1)}, f32[4608]{0:T(1024)}, u32[]{:S(2)}) copy-start(f32[4608]{0:T(1024)} %param.13) | copy-start | bytes 55300
